TPU v7x, 512 devices: a whole 4x8x8 slice. The times are simulated.
512 devices in a mesh: ctx: 32 (over z, x), head: 16 (over y, core).
Axes of the slice: x: 4, y: 8, z: 8, core: 2. Of those that a mesh axis runs over, the one named last changes fastest.
Arguments:
- queries: bfloat16 [8192, 4096], P('ctx', 'head'), may hold values from -5 to 5
- keys: bfloat16 [8192, 4096], P('ctx', 'head'), may hold values from -5 to 5
- values: bfloat16 [8192, 4096], P('ctx', 'head'), may hold values from -6 to 6
- grad_out: bfloat16 [8192, 4096], P('ctx', 'head'), may hold values from -6 to 6
- out_weight: bfloat16 [4096, 4096], P(None, 'head'), may hold values from -0.09375 to 0.09375
- doc_lengths: int32 [16], replicated, may hold values from 1 to 513, 8192 in all
- strata: int32 [16], replicated, may hold values from 0 to 7
- mask_level: int32 [8192], P('ctx'), may hold values from 0 to 7
Outputs:
- query_grad: bfloat16 [8192, 4096], P('ctx', 'head')
- key_grad: bfloat16 [8192, 4096], P('ctx', 'head')
- value_grad: bfloat16 [8192, 4096], P('ctx', 'head')
- out_weight_grad: float32 [4096, 4096], P('ctx', 'head')
Inputs may be any that keep to these rules, and one draw needn't show every extreme that they name: `doc_lengths`: the lengths sum to 8192; the longest document has exactly 513 tokens.
All inputs are finite; a program needn't handle non-finite values.
Results may differ from a plain program's by a relative error of at most 0.011.
Values may be sent and summed in bfloat16 or wider, within the bound.
A program may use at most 64 MiB of HBM per device.

v0:
```python
import jax
import jax.numpy as jnp
from jax import lax
from jax.sharding import PartitionSpec as P

HD = 128
STRATA = 8


def padded(block, sides, width):
    for axis, dim in sides:
        count = lax.axis_size(axis)
        forward = [(i, i + 1) for i in range(count - 1)]
        backward = [(target, source) for source, target in forward]
        low = lax.ppermute(
            lax.slice_in_dim(block, block.shape[dim] - width, None, axis=dim), axis, forward
        )
        high = lax.ppermute(lax.slice_in_dim(block, 0, width, axis=dim), axis, backward)
        block = jnp.concatenate([low, block, high], axis=dim)
    return block


def passed_along(block, axis, distance):
    devices = range(lax.axis_size(axis))
    route = [(i - distance, i) for i in devices if i - distance in devices]
    return lax.ppermute(block, axis, route)


def document_ids(doc_ends, first, count):
    positions = first + jnp.arange(count, dtype=jnp.int32)
    counted = jnp.sum((doc_ends[None, :] <= positions[:, None]).astype(jnp.int32), axis=1)
    within = (positions >= 0) & (positions < doc_ends[-1])
    return jnp.where(within, counted, -1)


def intersections(first_docs, second_docs):
    return jnp.maximum(jnp.min(first_docs), jnp.min(second_docs)) <= jnp.minimum(
        jnp.max(first_docs), jnp.max(second_docs)
    )


def two_shard_window(block, extend):
    row_count = block.shape[0]
    inner = extend(block)
    outward = jnp.concatenate([inner[2 * row_count :], inner[:row_count]], axis=0)
    outer = extend(outward)
    return jnp.concatenate([outer[:row_count], inner, outer[3 * row_count :]], axis=0)


def attend(query_heads, grad_heads, query_docs, key_heads, value_heads, key_docs):
    row_count, head_count, head_size = query_heads.shape
    score_scale = head_size ** (-0.5)
    tile_count = key_heads.shape[0] // row_count
    piece_width = 2 * head_count * head_size

    def tile_scores(key_tile, tile_docs):
        scores = (
            jnp.einsum("qhd,khd->hqk", query_heads, key_tile, preferred_element_type=jnp.float32)
            * score_scale
        )
        same_doc = (query_docs[:, None] == tile_docs[None, :])[None]
        return (jnp.where(same_doc, scores, -1e30), same_doc)

    tiles = []
    for index in range(tile_count):
        lower = index * row_count
        tiles.append(
            (
                key_heads[lower : lower + row_count],
                value_heads[lower : lower + row_count],
                key_docs[lower : lower + row_count],
            )
        )
    running_max = jnp.full((head_count, row_count), -1e30, jnp.float32)
    running_sum = jnp.zeros((head_count, row_count), jnp.float32)
    for key_tile, value_tile, tile_docs in tiles:

        def update(state_pair, key_tile=key_tile, tile_docs=tile_docs):
            old_max, old_sum = state_pair
            masked_scores, same_doc = tile_scores(key_tile, tile_docs)
            new_max = jnp.maximum(old_max, jnp.max(masked_scores, axis=2))
            fresh_terms = jnp.where(same_doc, jnp.exp(masked_scores - new_max[:, :, None]), 0.0)
            return (new_max, old_sum * jnp.exp(old_max - new_max) + jnp.sum(fresh_terms, axis=2))

        running_max, running_sum = lax.cond(
            intersections(query_docs, tile_docs),
            update,
            lambda state_pair: state_pair,
            (running_max, running_sum),
        )
    log_norm = running_max + jnp.log(running_sum)
    output = jnp.zeros((head_count, row_count, head_size), jnp.float32)
    for key_tile, value_tile, tile_docs in tiles:

        def accumulate(output, key_tile=key_tile, value_tile=value_tile, tile_docs=tile_docs):
            masked_scores, same_doc = tile_scores(key_tile, tile_docs)
            attention_half = jnp.exp(masked_scores - log_norm[:, :, None]).astype(jnp.bfloat16)
            return output + jnp.einsum(
                "hqk,khd->hqd", attention_half, value_tile, preferred_element_type=jnp.float32
            )

        output = lax.cond(
            intersections(query_docs, tile_docs), accumulate, lambda output: output, output
        )
    correction = jnp.sum(grad_heads.astype(jnp.float32).transpose(1, 0, 2) * output, axis=2)
    query_sum = jnp.zeros((row_count, head_count, head_size), jnp.float32)
    partials = {}
    for index in range(tile_count):
        key_tile, value_tile, tile_docs = tiles[index]

        def backward(
            query_sum, key_tile=key_tile, value_tile=value_tile, tile_docs=tile_docs, index=index
        ):
            masked_scores, same_doc = tile_scores(key_tile, tile_docs)
            attention = jnp.exp(masked_scores - log_norm[:, :, None])
            dot_grad = jnp.einsum(
                "qhd,khd->hqk", grad_heads, value_tile, preferred_element_type=jnp.float32
            )
            score_grad = (attention * (dot_grad - correction[:, :, None]) * score_scale).astype(
                jnp.bfloat16
            )
            query_sum = query_sum + jnp.einsum(
                "hqk,khd->qhd", score_grad, key_tile, preferred_element_type=jnp.float32
            )
            key_part = jnp.einsum(
                "hqk,qhd->khd", score_grad, query_heads, preferred_element_type=jnp.float32
            )
            value_part = jnp.einsum(
                "hqk,qhd->khd",
                attention.astype(jnp.bfloat16),
                grad_heads,
                preferred_element_type=jnp.float32,
            )
            key_piece = jnp.concatenate(
                [key_part.reshape(row_count, -1), value_part.reshape(row_count, -1)], axis=1
            )
            return (query_sum, key_piece)

        def skipped(query_sum):
            return (query_sum, jnp.zeros((row_count, piece_width), jnp.float32))

        query_sum, partials[index] = lax.cond(
            intersections(query_docs, tile_docs), backward, skipped, query_sum
        )
    return (query_sum.reshape(row_count, -1), partials, output)


def local(queries, keys, values, grad_out, out_weight, doc_lengths, strata, mask_level):
    row_count, columns = queries.shape
    head_count = columns // HD
    shard_index = lax.axis_index("ctx")
    doc_ends = jnp.cumsum(doc_lengths)
    own_docs = document_ids(doc_ends, shard_index * row_count, row_count)
    window_docs = document_ids(doc_ends, (shard_index - 2) * row_count, 5 * row_count)
    doc_table = (
        own_docs[:, None] == jnp.arange(doc_lengths.shape[0], dtype=jnp.int32)[None, :]
    ).astype(jnp.int32)
    stratum = jnp.sum(doc_table * strata[None, :], axis=1)
    token_weight = (mask_level < stratum + 1).astype(jnp.float32) * (
        STRATA / (stratum + 1).astype(jnp.float32)
    )
    gathered = lax.all_gather(grad_out, "head", axis=1, tiled=True)
    attn_grad = (
        token_weight[:, None] * jnp.dot(gathered, out_weight, preferred_element_type=jnp.float32)
    ).astype(jnp.bfloat16)
    query_heads = queries.reshape(row_count, head_count, HD)
    grad_heads = attn_grad.reshape(row_count, head_count, HD)

    def extend_pairs(block):
        return padded(block, (("ctx", 0),), row_count)

    window = two_shard_window(jnp.concatenate([keys, values], axis=1), extend_pairs)
    key_heads = window[:, :columns].reshape(5 * row_count, head_count, HD)
    value_heads = window[:, columns:].reshape(5 * row_count, head_count, HD)
    query_sum, partials, output = attend(
        query_heads, grad_heads, own_docs, key_heads, value_heads, window_docs
    )
    key_total = partials[2]
    for offset in (-2, -1, 1, 2):
        key_total = key_total + passed_along(partials[2 + offset], "ctx", offset)
    scaled_out = (
        token_weight[:, None] * output.transpose(1, 0, 2).reshape(row_count, columns)
    ).astype(jnp.bfloat16)
    weight_grad = lax.psum_scatter(
        lax.dot_general(
            gathered, scaled_out, (((0,), (0,)), ((), ())), preferred_element_type=jnp.float32
        ),
        "ctx",
        scatter_dimension=0,
        tiled=True,
    )
    return (
        query_sum.astype(jnp.bfloat16),
        key_total[:, :columns].astype(jnp.bfloat16),
        key_total[:, columns:].astype(jnp.bfloat16),
        weight_grad,
    )


def solution(mesh):
    placed = (
        P("ctx", "head"),
        P("ctx", "head"),
        P("ctx", "head"),
        P("ctx", "head"),
        P(None, "head"),
        P(),
        P(),
        P("ctx"),
    )
    return jax.shard_map(
        local,
        mesh=mesh,
        in_specs=placed,
        out_specs=(P("ctx", "head"), P("ctx", "head"), P("ctx", "head"), P("ctx", "head")),
        check_vma=False,
    )
```

profile of v0, /device:TPU:16, one launch (start us, length us, event | category | flops | bytes accessed | tf_op | source)
XLA Modules:
  0.0 339.8 jit_solution(5044535710021414916)
XLA Ops:
  7.2 0.7 all-gather.2.cloned.1.call-update
  8.0 1.0 copy.120
  9.0 1.0 copy.121
  10.0 1.3 collective-permute-start.2
  11.3 4.6 %collective-permute-start = (bf16[256,512]{0,1:T(8,128)(2,1)S(1)}, bf16[256,512]{0,1:T(8,128)(2,1)S(1)}, u32[]{:S(2)}, u32[]{:S(2)}) collective-permute-start(bf16[256,512]{0,1:T(8,128)(2,1)S(1)} %pad_maximum_fusion.5), channel_id=1, source_target_pairs={{0,16},{16,32},{32,48},{48,64},{64,80},{80,96},{96,112},{112,128},... | collective-permute-start | bytes 786440 | tf_op jit(solution)/shard_map/ppermute | solution.py:15
  15.9 0.7 copy.118
  17.5 1.3 fusion.111
  18.8 0.6 and_select_fusion
  19.4 1.4 slice_reduce_fusion
  20.9 0.7 select_reduce_fusion.5
  34.3 1.0 copy.119
  35.3 1.3 compare_select_fusion
  36.6 3.4 collective-permute-start.1
  40.0 1.3 collective-permute-start.3
  41.3 0.7 fusion.120
  42.0 2.9 collective-permute-done.1
  44.9 0.7 fusion.121
  45.6 0.6 conditional.15
  46.2 2.5 conditional.17
  46.6 0.7 max.4
  47.4 0.7 multiply_add_fusion.2
  48.1 0.6 copy.227
  48.7 2.5 conditional.18
  49.1 0.7 max.5
  49.9 0.7 multiply_add_fusion.3
  50.5 0.6 copy.231
  51.1 1.6 fusion.118
  52.8 2.5 conditional.19
  53.2 0.7 max.7
  54.0 0.7 multiply_add_fusion.4
  55.2 0.7 log_add_fusion
  56.6 1.8 conditional.23
  56.6 0.6 copy-done.14
  57.3 1.1 fusion.45
  58.4 1.5 conditional.24
  58.6 1.3 fusion.57
  60.1 4.2 %convolution_bitcast_fusion.5 = f32[4096,256]{0,1:T(8,128)} fusion(bf16[256,256]{0,1:T(8,128)(2,1)S(1)} %fusion.109, bf16[256,4096]{1,0:T(8,128)(2,1)} %all-gather.2.cloned.1.call-done), kind=kOutput, calls=%fused_computation.164 | convolution fusion | flops 536870912 | bytes 6422528 | tf_op jit(solution)/shard_map/dot_general | solution.py:185
  64.6 2.6 fusion.108
  67.3 1.0 copy.161
  68.3 1.0 copy.163
  69.4 4.7 %conditional.27 = (f32[256,2,128]{2,0,1:T(8,128)S(1)}, f32[256,512]{1,0:T(8,128)}) conditional(s32[]{:T(128)} %convert_element_type.100, f32[256,2,128]{2,0,1:T(8,128)S(1)} %get-tuple-element.402, (s32[256]{0:T(256)S(1)}, s32[256]{0:T(256)}, bf16[256,2,128]{0,2,1:T(8,128)(2,1)S(1)}, bf16[256,2,128]{0,2,1:T(8,128)(2,1)S(1)}, f32[2,256]{1,0:T(2,128)}, ...), branch_computations={%region_51.52_spmd, %region_52.53_spmd} | conditional | flops 169082880 | bytes 6559760 | solution.py:142
  69.4 0.8 broadcast_compare_fusion.12
  70.2 1.0 fusion.83
  71.2 1.2 fusion.86
  73.0 1.0 copy.214
  74.0 2.1 conditional.28
  74.2 1.0 fusion.92
  76.1 1.0 copy.164
  77.1 3.0 conditional.29
  77.2 1.0 fusion.101
  78.2 1.2 fusion.104
  80.1 1.0 copy.165
  81.1 12.0 %collective-permute-start.7 = (f32[256,512]{1,0:T(8,128)}, f32[256,512]{1,0:T(8,128)S(1)}, u32[]{:S(2)}, u32[]{:S(2)}) collective-permute-start(f32[256,512]{1,0:T(8,128)} %copy.165), channel_id=1, source_target_pairs={{0,32},{16,48},{32,64},{48,80},{64,96},{80,112},{96,128},{112,144}... | collective-permute-start | bytes 1572872 | tf_op jit(solution)/shard_map/ppermute | solution.py:26
  93.1 6.1 %collective-permute-start.6 = (f32[256,512]{1,0:T(8,128)}, f32[256,512]{1,0:T(8,128)S(1)}, u32[]{:S(2)}, u32[]{:S(2)}) collective-permute-start(f32[256,512]{1,0:T(8,128)} %copy.164), channel_id=1, source_target_pairs={{0,16},{16,32},{32,48},{48,64},{64,80},{80,96},{96,112},{112,128},... | collective-permute-start | bytes 1572872 | tf_op jit(solution)/shard_map/ppermute | solution.py:26
  99.2 1.3 collective-permute-start.5
  100.5 1.3 collective-permute-start.4
  101.8 0.7 copy_bitcast_fusion
  102.5 3.9 %collective-permute-done.7 = f32[256,512]{1,0:T(8,128)S(1)} collective-permute-done((f32[256,512]{1,0:T(8,128)}, f32[256,512]{1,0:T(8,128)S(1)}, u32[]{:S(2)}, u32[]{:S(2)}) %collective-permute-start.7) | collective-permute-done | bytes 524320 | tf_op jit(solution)/shard_map/ppermute | solution.py:26
  106.4 10.0 %collective-permute-done.6 = f32[256,512]{1,0:T(8,128)S(1)} collective-permute-done((f32[256,512]{1,0:T(8,128)}, f32[256,512]{1,0:T(8,128)S(1)}, u32[]{:S(2)}, u32[]{:S(2)}) %collective-permute-start.6) | collective-permute-done | bytes 524320 | tf_op jit(solution)/shard_map/ppermute | solution.py:26
  116.4 24.8 %collective-permute-done.5 = f32[256,512]{1,0:T(8,128)S(1)} collective-permute-done((f32[256,512]{1,0:T(8,128)}, f32[256,512]{1,0:T(8,128)S(1)}, u32[]{:S(2)}, u32[]{:S(2)}) %collective-permute-start.5) | collective-permute-done | bytes 524320 | tf_op jit(solution)/shard_map/ppermute | solution.py:26
  141.3 1.3 add_convert_fusion
  142.5 0.7 fusion.117
  143.3 188.0 %reduce-scatter.2.cloned.1.call-done = f32[128,256]{0,1:T(8,128)} async-done(((f32[4096,256]{0,1:T(8,128)}), f32[128,256]{0,1:T(8,128)}) %reduce-scatter.2.cloned.1.call-update) | async-done | bytes 131088 | tf_op jit(solution)/shard_map/reduce_scatter | solution.py:184
  331.3 1.7 copy.167
  (91 shorter events, 8.1 us)
Async XLA Ops:
  7.2 57.4 %copy-start = (bf16[4096,256]{1,0:T(8,128)(2,1)S(1)}, bf16[4096,256]{1,0:T(8,128)(2,1)}, u32[]{:S(2)}) copy-start(bf16[4096,256]{1,0:T(8,128)(2,1)} %param.42) | copy-start | bytes 6291460
  7.2 52.9 %all-gather.2.cloned.1.call-start = ((), (), s32[]{:S(2)}) async-start(), calls=%async_computation.1 | async-start | bytes 2228224 | tf_op jit(solution)/shard_map/all_gather | solution.py:162
  7.9 323.4 %reduce-scatter.2.cloned.1.call-start = ((), (), s32[]{:S(2)}) async-start(), calls=%async_computation.2 | async-start | bytes 4325376 | tf_op jit(solution)/shard_map/reduce_scatter | solution.py:184
  10.0 46.0 %copy-start.3 = (bf16[256,256]{0,1:T(8,128)(2,1)}, bf16[256,256]{0,1:T(8,128)(2,1)S(1)}, u32[]{:S(2)}) copy-start(bf16[256,256]{0,1:T(8,128)(2,1)S(1)} %copy.121) | copy-start | bytes 393220
  10.0 30.0 %collective-permute-start.2 = (bf16[256,512]{0,1:T(8,128)(2,1)S(1)}, bf16[256,512]{0,1:T(8,128)(2,1)S(1)}, u32[]{:S(2)}, u32[]{:S(2)}) collective-permute-start(bf16[256,512]{0,1:T(8,128)(2,1)S(1)} %pad_maximum_fusion.5), channel_id=1, source_target_pairs={{16,0},{32,16},{48,32},{64,48},{80,64},{96,80},{112,96},{128,112},... | collective-permute-start | bytes 786440 | tf_op jit(solution)/shard_map/ppermute | solution.py:18
  11.3 25.3 %collective-permute-start = (bf16[256,512]{0,1:T(8,128)(2,1)S(1)}, bf16[256,512]{0,1:T(8,128)(2,1)S(1)}, u32[]{:S(2)}, u32[]{:S(2)}) collective-permute-start(bf16[256,512]{0,1:T(8,128)(2,1)S(1)} %pad_maximum_fusion.5), channel_id=1, source_target_pairs={{0,16},{16,32},{32,48},{48,64},{64,80},{80,96},{96,112},{112,128},... | collective-permute-start | bytes 786440 | tf_op jit(solution)/shard_map/ppermute | solution.py:15
  20.9 35.1 %copy-start.7 = (s32[256]{0:T(256)}, s32[256]{0:T(256)S(1)}, u32[]{:S(2)}) copy-start(s32[256]{0:T(256)S(1)} %get-tuple-element.738) | copy-start | bytes 3076
  36.6 8.4 %collective-permute-start.1 = (bf16[256,512]{0,1:T(8,128)(2,1)S(1)}, bf16[256,512]{0,1:T(8,128)(2,1)S(1)}, u32[]{:S(2)}, u32[]{:S(2)}) collective-permute-start(bf16[256,512]{0,1:T(8,128)(2,1)S(1)} %collective-permute-done), channel_id=1, source_target_pairs={{0,16},{16,32},{32,48},{48,64},{64,80},{80,96},{96,112},{112,128},... | collective-permute-start | bytes 786440 | tf_op jit(solution)/shard_map/ppermute | solution.py:15
  40.0 6.2 %copy-start.8 = (s32[256]{0:T(256)S(1)}, s32[256]{0:T(256)}, u32[]{:S(2)}) copy-start(s32[256]{0:T(256)} %get-tuple-element.739) | copy-start | bytes 3076
  40.0 16.5 %copy-start.4 = (bf16[256,256]{0,1:T(8,128)(2,1)}, bf16[256,256]{0,1:T(8,128)(2,1)S(1)}, u32[]{:S(2)}) copy-start(bf16[256,256]{0,1:T(8,128)(2,1)S(1)} %get-tuple-element.730) | copy-start | bytes 393220
  40.0 11.1 %collective-permute-start.3 = (bf16[256,512]{0,1:T(8,128)(2,1)S(1)}, bf16[256,512]{0,1:T(8,128)(2,1)}, u32[]{:S(2)}, u32[]{:S(2)}) collective-permute-start(bf16[256,512]{0,1:T(8,128)(2,1)S(1)} %collective-permute-done.2), channel_id=1, source_target_pairs={{16,0},{32,16},{48,32},{64,48},{80,64},{96,80},{112,96},{128,112},... | collective-permute-start | bytes 786440 | tf_op jit(solution)/shard_map/ppermute | solution.py:18
  48.7 7.2 %copy-start.9 = (s32[256]{0:T(256)S(1)}, s32[256]{0:T(256)}, u32[]{:S(2)}) copy-start(s32[256]{0:T(256)} %get-tuple-element.740) | copy-start | bytes 3076
  52.8 5.7 %copy-start.1 = (bf16[256,256]{0,1:T(8,128)(2,1)}, bf16[256,256]{0,1:T(8,128)(2,1)S(1)}, u32[]{:S(2)}) copy-start(bf16[256,256]{0,1:T(8,128)(2,1)S(1)} %get-tuple-element.729) | copy-start | bytes 393220
  55.9 0.7 copy-start.12
  56.5 3.5 %copy-start.11 = (f32[256]{0:T(256)S(1)}, f32[256]{0:T(256)}, u32[]{:S(2)}) copy-start(f32[256]{0:T(256)} %compare_select_fusion) | copy-start | bytes 3076
  56.6 0.6 copy-start.14
  64.5 2.6 copy-start.6
  64.5 2.6 copy-start.10
  64.5 2.6 copy-start.13
  69.4 4.7 %copy-start.5 = (bf16[256,256]{0,1:T(8,128)(2,1)S(1)}, bf16[256,256]{0,1:T(8,128)(2,1)}, u32[]{:S(2)}) copy-start(bf16[256,256]{0,1:T(8,128)(2,1)} %copy-done.4) | copy-start | bytes 393220
  74.0 3.1 copy-start.2
  81.1 25.3 %collective-permute-start.7 = (f32[256,512]{1,0:T(8,128)}, f32[256,512]{1,0:T(8,128)S(1)}, u32[]{:S(2)}, u32[]{:S(2)}) collective-permute-start(f32[256,512]{1,0:T(8,128)} %copy.165), channel_id=1, source_target_pairs={{0,32},{16,48},{32,64},{48,80},{64,96},{80,112},{96,128},{112,144}... | collective-permute-start | bytes 1572872 | tf_op jit(solution)/shard_map/ppermute | solution.py:26
  93.1 23.3 %collective-permute-start.6 = (f32[256,512]{1,0:T(8,128)}, f32[256,512]{1,0:T(8,128)S(1)}, u32[]{:S(2)}, u32[]{:S(2)}) collective-permute-start(f32[256,512]{1,0:T(8,128)} %copy.164), channel_id=1, source_target_pairs={{0,16},{16,32},{32,48},{48,64},{64,80},{80,96},{96,112},{112,128},... | collective-permute-start | bytes 1572872 | tf_op jit(solution)/shard_map/ppermute | solution.py:26
  99.2 42.1 %collective-permute-start.5 = (f32[256,512]{1,0:T(8,128)}, f32[256,512]{1,0:T(8,128)S(1)}, u32[]{:S(2)}, u32[]{:S(2)}) collective-permute-start(f32[256,512]{1,0:T(8,128)} %copy.163), channel_id=1, source_target_pairs={{16,0},{32,16},{48,32},{64,48},{80,64},{96,80},{112,96},{128,112},... | collective-permute-start | bytes 1572872 | tf_op jit(solution)/shard_map/ppermute | solution.py:26
  100.5 40.8 %collective-permute-start.4 = (f32[256,512]{1,0:T(8,128)}, f32[256,512]{1,0:T(8,128)S(1)}, u32[]{:S(2)}, u32[]{:S(2)}) collective-permute-start(f32[256,512]{1,0:T(8,128)} %copy.161), channel_id=1, source_target_pairs={{32,0},{48,16},{64,32},{80,48},{96,64},{112,80},{128,96},{144,112}... | collective-permute-start | bytes 1572872 | tf_op jit(solution)/shard_map/ppermute | solution.py:26
Sparse Core Ops, SparseCore 0:
  10.1 47.3 all-gather.1
  64.5 266.7 reduce-scatter.1
where the time goes:
time: 341 us; the launch traced here: 340 us
  waiting for transfers between devices  230 us (67%)
  starting transfers between devices  31.3 us (9%)
  between operations  27.1 us (8%)
  local copies, waits for them, and re-layouts  18 us (5%)
  matrix products  18 us (5%)
  other arithmetic  14.6 us (4%)
    reduce_scatter x1, waiting for transfers between devices, local(): lax.psum_scatter(lax.dot_general(gathered, scaled_out, (((0,), (0,)), (()...  188 us
    ppermute x4, waiting for transfers between devices, passed_along(): return lax.ppermute(block, axis, route)  38.8 us
    ppermute x4, starting transfers between devices, passed_along(): return lax.ppermute(block, axis, route)  20.7 us
    ppermute x2, starting transfers between devices, padded(): lax.ppermute(lax.slice_in_dim(block, block.shape[dim] - width, None, axis...  7.95 us
  transfers between devices with their start and end apart: 10, of which 5 were waited for; matrix products, arithmetic and copies ran while one was open for 13% of the time, Pallas kernels for 0%

commit v1 on v0

v1 whole, which is shorter than its diff:
```python
import jax
import jax.numpy as jnp
from jax import lax
from jax.experimental import pallas as pl
from jax.experimental.pallas import tpu as pltpu
from jax.sharding import PartitionSpec as P

HD = 128
STRATA = 8
MESH = pl.DeviceIdType.MESH
NZ, NX, NY = 8, 4, 8
TOK = 256
COLS = 256
HALO = 16
EXT = TOK + HALO
KEYS = 640
NEG = -1e30

NT = (((1,), (1,)), ((), ()))
TN = (((0,), (0,)), ((), ()))
F32 = jnp.float32
BF16 = jnp.bfloat16


def dot(a, b, dims=(((1,), (0,)), ((), ()))):
    return lax.dot_general(a, b, dims, preferred_element_type=F32)


def kernel(
    q_hbm, k_hbm, v_hbm, g_hbm, w_hbm, len_ref, strata_ref, level_ref,
    dq_out, dk_out, dv_out, dw_out,
    q_all, k_all, v_all, g_all, gt, w_all, dacc, do_all, p_all, o_all, s_all,
    dq_all, dkv_own, o_ret, ret1, ret1_in, ret2, ret2_in, part, part_in,
    p_up, p_dn, zs, zr, red, xs, xr,
    local_sem, ag_send, ag_recv, sib_send, sib_recv, kv_send, kv_recv,
    ret_send, ret_recv, z_send, z_recv, x_send, x_recv,
):
    c = lax.axis_index("ctx")
    h = lax.axis_index("head")
    z, x, y, core = c // NX, c % NX, h // 2, h % 2
    side = c % 2
    sign = 2 * side - 1
    edge = pl.multiple_of(side * (TOK - HALO), HALO)

    def at_ctx(index):
        return {"ctx": (index + NZ * NX) % (NZ * NX), "head": h}

    def at_zx(zz, xx):
        return {"ctx": (zz + NZ) % NZ * NX + (xx + NX) % NX, "head": h}

    def at_y(yy):
        return {"ctx": c, "head": (yy + NY) % NY * 2 + core}

    y_up, y_dn = at_y(y + 1), at_y(y - 1)
    z_up, z_dn = at_zx(z + 1, x), at_zx(z - 1, x)
    x_up, x_dn = at_zx(z, x + 1), at_zx(z, x - 1)
    sibling = {"ctx": c, "head": h + 1 - 2 * core}
    partner = at_ctx(c - sign)
    mirror = at_ctx(c + sign)
    far_to, far_from = at_ctx(c + 2 * sign), at_ctx(c - 2 * sign)

    def remote(src, dst, ssem, rsem, device):
        return pltpu.make_async_remote_copy(
            src_ref=src, dst_ref=dst, send_sem=ssem, recv_sem=rsem, device_id=device, device_id_type=MESH
        )

    own = [
        pltpu.make_async_copy(src, dst, local_sem.at[n])
        for n, (src, dst) in enumerate(
            [
                (g_hbm, g_all.at[0, 0]),
                (q_hbm, q_all.at[pl.ds(0, TOK)]),
                (k_hbm, k_all.at[pl.ds(0, TOK)]),
                (v_hbm, v_all.at[pl.ds(0, TOK)]),
                (w_hbm, w_all),
            ]
        )
    ]
    for copy in own:
        copy.start()

    barrier = pltpu.get_barrier_semaphore()
    greeted = [y_up, y_dn, z_up, z_dn, x_up, x_dn, sibling, partner, mirror, far_to, far_from]
    for device in greeted:
        pl.semaphore_signal(barrier, inc=1, device_id=device, device_id_type=MESH)

    doc = c // 2
    position = c * TOK + lax.broadcasted_iota(jnp.int32, (1, TOK), 1)
    stratum = jnp.zeros((1, TOK), jnp.int32)
    begin = jnp.int32(0)
    doc_begin = jnp.int32(0)
    doc_end = jnp.int32(0)
    for n in range(16):
        finish = begin + len_ref[n]
        within = (position >= begin) & (position < finish)
        stratum = jnp.where(within, strata_ref[n], stratum)
        doc_begin = jnp.where(doc == n, begin, doc_begin)
        doc_end = jnp.where(doc == n, finish, doc_end)
        begin = finish
    level = level_ref[...].reshape(1, TOK)
    weight_row = jnp.where(level < stratum + 1, STRATA / (stratum + 1).astype(F32), 0.0)
    weight = jnp.transpose(jnp.broadcast_to(weight_row, (HD, TOK)))

    other = 1 - side

    def place(index, own_first, halo_first):
        return jnp.where(index < TOK, own_first + index, halo_first + index - TOK)

    own_first = c * TOK
    own_halo = own_first - HALO + (TOK + HALO) * side
    partner_first = (c - sign) * TOK
    partner_halo = partner_first - HALO + (TOK + HALO) * other
    rows = place(lax.broadcasted_iota(jnp.int32, (EXT, 1), 0), own_first, own_halo)
    row_in = ((rows >= doc_begin) & (rows < doc_end)).astype(F32)
    lane = lax.broadcasted_iota(jnp.int32, (1, KEYS), 1)
    keys_at = jnp.where(
        lane < TOK,
        own_first + lane,
        jnp.where(
            lane < 2 * TOK,
            partner_first + lane - TOK,
            jnp.where(lane < 2 * TOK + HALO, own_halo + lane - 2 * TOK, partner_halo + lane - 2 * TOK - HALO),
        ),
    )
    key_in = (keys_at >= doc_begin) & (keys_at < doc_end) & (lane < 2 * TOK + 2 * HALO)
    bias = jnp.where(key_in, 0.0, NEG)
    pad = KEYS - 2 * TOK - 2 * HALO
    k_all[pl.ds(KEYS - pad, pad), :] = jnp.zeros((pad, COLS), BF16)
    v_all[pl.ds(KEYS - pad, pad), :] = jnp.zeros((pad, COLS), BF16)

    pl.semaphore_wait(barrier, len(greeted))

    half = TOK // 2

    def ag_copy(up, s, part_index, from_own):
        rows_of = pl.ds(part_index * half, half)
        direction = 0 if up else 1
        slot_here = (NY - (s - 1)) % NY if up else s - 1
        slot_there = NY - s if up else s
        src = g_hbm.at[rows_of] if from_own else g_all.at[slot_here, 0, rows_of]
        index = direction * 8 + (s - 1) * 2 + part_index
        return remote(
            src, g_all.at[slot_there, 0, rows_of], ag_send.at[index], ag_recv.at[index], y_up if up else y_dn
        )

    def sib_copy(slot, part_index, from_own=False):
        rows_of = pl.ds(part_index * half, half)
        src = g_hbm.at[rows_of] if from_own else g_all.at[slot, 0, rows_of]
        index = slot * 2 + part_index
        return remote(src, g_all.at[slot, 1, rows_of], sib_send.at[index], sib_recv.at[index], sibling)

    ag = {}
    sib = {}
    for part_index in range(2):
        for up in (True, False):
            ag[up, 1, part_index] = ag_copy(up, 1, part_index, True)
            ag[up, 1, part_index].start()
    kv = [
        remote(k_hbm, k_all.at[pl.ds(TOK, TOK)], kv_send.at[0], kv_recv.at[0], partner),
        remote(v_hbm, v_all.at[pl.ds(TOK, TOK)], kv_send.at[1], kv_recv.at[1], partner),
    ]
    rim = pl.ds(edge, HALO)
    for n, (src, dst, device) in enumerate(
        [
            (k_hbm, k_all.at[pl.ds(2 * TOK, HALO)], mirror),
            (v_hbm, v_all.at[pl.ds(2 * TOK, HALO)], mirror),
            (q_hbm, q_all.at[pl.ds(TOK, HALO)], mirror),
            (k_hbm, k_all.at[pl.ds(2 * TOK + HALO, HALO)], far_to),
            (v_hbm, v_all.at[pl.ds(2 * TOK + HALO, HALO)], far_to),
        ]
    ):
        kv.append(remote(src.at[rim], dst, kv_send.at[2 + n], kv_recv.at[2 + n], device))
    for copy in kv[2:] + kv[:2]:
        copy.start()
    for part_index in range(2):
        sib[0, part_index] = sib_copy(0, part_index, True)
        sib[0, part_index].start()

    def take_block(slot, r):
        index = (y + slot) % NY * 2 + (core + r) % 2
        first = pl.multiple_of(index * COLS, COLS)
        block = g_all[slot, r]
        gt[pl.ds(first, COLS), :] = jnp.transpose(block)

    for copy in own:
        copy.wait()
    take_block(0, 0)
    for part_index in range(2):
        sib[0, part_index].wait_recv()
    take_block(0, 1)

    for s in range(1, NY // 2):
        for part_index in range(2):
            for up in (True, False):
                ag[up, s, part_index].wait_recv()
                if s + 1 < NY // 2 or part_index == (0 if up else 1):
                    ag[up, s + 1, part_index] = ag_copy(up, s + 1, part_index, False)
                    ag[up, s + 1, part_index].start()
                slot = NY - s if up else s
                sib[slot, part_index] = sib_copy(slot, part_index)
                sib[slot, part_index].start()
        for slot in (s, NY - s):
            take_block(slot, 0)
        if s > 1:
            for slot in (s - 1, NY - s + 1):
                for part_index in range(2):
                    sib[slot, part_index].wait_recv()
                take_block(slot, 1)

    scale = HD**-0.5
    for copy in kv:
        copy.wait_recv()
    for n in range(2):
        cols = pl.ds(n * HD, HD)
        scores = dot(q_all[:, cols], k_all[:, cols], NT) * scale + bias
        top = jnp.max(scores, axis=1, keepdims=True)
        terms = jnp.exp(scores - top)
        total = jnp.sum(terms, axis=1, keepdims=True)
        attention = terms * (row_in / total)
        p_all[n] = attention
        o_all[:, cols] = dot(attention.astype(BF16), v_all[:, cols])
    back = remote(o_all.at[pl.ds(TOK, HALO)], o_ret, ret_send.at[0], ret_recv.at[0], mirror)
    back.start()

    last = NY // 2
    for up in (True, False):
        part_index = 0 if up else 1
        ag[up, last, part_index].wait_recv()
        sib[last, part_index] = sib_copy(last, part_index)
        sib[last, part_index].start()
    for slot in (last - 1, last + 1):
        for part_index in range(2):
            sib[slot, part_index].wait_recv()
        take_block(slot, 1)
    take_block(last, 0)
    for part_index in range(2):
        sib[last, part_index].wait_recv()
    take_block(last, 1)

    back.wait_recv()
    s_all[...] = o_all[pl.ds(0, TOK), :]
    s_all[rim, :] += o_ret[...]
    for n in range(2):
        cols = pl.ds(n * HD, HD)
        s_all[:, cols] = s_all[:, cols] * weight
    scaled = s_all[...].astype(BF16)

    spots = [(x + 2) % NX, (x + 1) % NX, (x + NX - 1) % NX, x]
    DEST = 4096 // (NZ * NX)

    def z_block(zz):
        first = pl.multiple_of((zz + NZ) % NZ * (DEST * NX), DEST * NX)
        return dot(gt[pl.ds(first, DEST * NX), :], scaled)

    def rows_at(q):
        return pl.ds(pl.multiple_of(spots[q] * DEST, DEST), DEST)

    zc = {}

    def z_step(t):
        if t == 0:
            p_up[...] = z_block(z + 4)
        else:
            p_up[...] = z_block(z + 4 - t)
            p_dn[...] = z_block(z - 4 + t)
        for q in range(4):
            for up in (True, False):
                if t == 0 and (q < 2) != up:
                    continue
                source = p_up if up or t == 0 else p_dn
                value = source[rows_at(q), :]
                if (up, t - 1, q) in zc:
                    zc[up, t - 1, q].wait_recv()
                    value = value + zr[0 if up else 1, t - 1, q].astype(F32)
                d = 0 if up else 1
                zs[d, t, q] = value.astype(BF16)
                index = d * 16 + t * 4 + q
                zc[up, t, q] = remote(
                    zs.at[d, t, q], zr.at[d, t, q], z_send.at[index], z_recv.at[index], z_up if up else z_dn
                )
                zc[up, t, q].start()

    z_step(0)

    dacc[...] = jnp.zeros((TOK, COLS), F32)
    for slot in range(NY):
        for r in range(2):
            index = (y + slot) % NY * 2 + (core + r) % 2
            first = pl.multiple_of(index * COLS, COLS)
            dacc[...] += dot(g_all[slot, r], w_all[pl.ds(first, COLS), :])
    for n in range(2):
        cols = pl.ds(n * HD, HD)
        do_all[pl.ds(0, TOK), cols] = (dacc[:, cols] * weight).astype(BF16)
    halo_grad = remote(
        do_all.at[rim], do_all.at[pl.ds(TOK, HALO)], ret_send.at[1], ret_recv.at[1], mirror
    )
    halo_grad.start()

    z_step(1)

    halo_grad.wait_recv()

    def backward(n):
        cols = pl.ds(n * HD, HD)
        attention = p_all[n]
        grads = do_all[:, cols]
        correction = jnp.sum(grads.astype(F32) * o_all[:, cols], axis=1, keepdims=True)
        dots = dot(grads, v_all[:, cols], NT)
        score_grad = (attention * (dots - correction) * scale).astype(BF16)
        dq_all[:, cols] = dot(score_grad, k_all[:, cols])
        for which, value in enumerate(
            (dot(score_grad, q_all[:, cols], TN), dot(attention.astype(BF16), grads, TN))
        ):
            dkv_own[which, :, cols] = value[:TOK]
            part[which, :, cols] = value[TOK : 2 * TOK].astype(BF16)
            ret1[1 + which, :, cols] = value[2 * TOK : 2 * TOK + HALO]
            ret2[which, :, cols] = value[2 * TOK + HALO : 2 * TOK + 2 * HALO]

    backward(0)
    backward(1)
    ret1[0] = dq_all[pl.ds(TOK, HALO), :]
    returns = [
        remote(part, part_in, ret_send.at[2], ret_recv.at[2], partner),
        remote(ret1, ret1_in, ret_send.at[3], ret_recv.at[3], mirror),
        remote(ret2, ret2_in, ret_send.at[4], ret_recv.at[4], far_from),
    ]
    for copy in returns:
        copy.start()

    z_step(2)
    z_step(3)

    for copy in returns:
        copy.wait_recv()
    dq_all[rim, :] += ret1_in[0]
    dq_out[...] = dq_all[pl.ds(0, TOK), :].astype(BF16)
    for which, out in enumerate((dk_out, dv_out)):
        dkv_own[which, rim, :] += ret1_in[1 + which] + ret2_in[which]
        out[...] = (dkv_own[which] + part_in[which].astype(F32)).astype(BF16)

    p_up[...] = z_block(z)

    def z_sum(q):
        for up in (True, False):
            zc[up, 3, q].wait_recv()
        return p_up[rows_at(q), :] + zr[0, 3, q].astype(F32) + zr[1, 3, q].astype(F32)

    xc = []
    mid = DEST // 2
    red[0] = z_sum(0).astype(BF16)
    for n, (first, device) in enumerate(((0, x_up), (mid, x_dn))):
        here = pl.ds(first, mid)
        copy = remote(red.at[0, here], xr.at[n, here], x_send.at[n], x_recv.at[n], device)
        copy.start()
        xc.append(copy)
    for n, (first, device) in enumerate(((0, x_up), (mid, x_dn))):
        xs[...] = z_sum(1 + n)
        xc[n].wait_recv()
        here = pl.ds(first, mid)
        xs[here, :] += xr[n, here, :].astype(F32)
        red[1 + n] = xs[...].astype(BF16)
        copy = remote(red.at[1 + n], xr.at[2 + n], x_send.at[2 + n], x_recv.at[2 + n], device)
        copy.start()
        xc.append(copy)
    final = z_sum(3)
    for copy in xc[2:]:
        copy.wait_recv()
    dw_out[...] = final + xr[2].astype(F32) + xr[3].astype(F32)

    for copy in list(ag.values()) + list(sib.values()) + kv + [back, halo_grad] + returns + list(zc.values()) + xc:
        copy.wait_send()


def local(queries, keys, values, grad_out, out_weight, doc_lengths, strata, mask_level):
    hbm = pl.BlockSpec(memory_space=pl.ANY)
    smem = pl.BlockSpec(memory_space=pltpu.SMEM)
    vmem = pl.BlockSpec(memory_space=pltpu.VMEM)
    dma = pltpu.SemaphoreType.DMA
    V = pltpu.VMEM
    dest = 4096 // (NZ * NX)
    return pl.pallas_call(
        kernel,
        out_shape=[
            jax.ShapeDtypeStruct((TOK, COLS), BF16),
            jax.ShapeDtypeStruct((TOK, COLS), BF16),
            jax.ShapeDtypeStruct((TOK, COLS), BF16),
            jax.ShapeDtypeStruct((dest, COLS), F32),
        ],
        in_specs=[hbm] * 5 + [smem, smem, vmem],
        out_specs=[vmem] * 4,
        scratch_shapes=[
            V((EXT, COLS), BF16),
            V((KEYS, COLS), BF16),
            V((KEYS, COLS), BF16),
            V((NY, 2, TOK, COLS), BF16),
            V((4096, TOK), BF16),
            V((4096, COLS), BF16),
            V((TOK, COLS), F32),
            V((EXT, COLS), BF16),
            V((2, EXT, KEYS), F32),
            V((EXT, COLS), F32),
            V((TOK, COLS), F32),
            V((EXT, COLS), F32),
            V((2, TOK, COLS), F32),
            V((HALO, COLS), F32),
            V((3, HALO, COLS), F32),
            V((3, HALO, COLS), F32),
            V((2, HALO, COLS), F32),
            V((2, HALO, COLS), F32),
            V((2, TOK, COLS), BF16),
            V((2, TOK, COLS), BF16),
            V((dest * NX, COLS), F32),
            V((dest * NX, COLS), F32),
            V((2, 4, 4, dest, COLS), BF16),
            V((2, 4, 4, dest, COLS), BF16),
            V((3, dest, COLS), BF16),
            V((dest, COLS), F32),
            V((4, dest, COLS), BF16),
            dma((5,)),
            dma((16,)),
            dma((16,)),
            dma((16,)),
            dma((16,)),
            dma((7,)),
            dma((7,)),
            dma((5,)),
            dma((5,)),
            dma((32,)),
            dma((32,)),
            dma((4,)),
            dma((4,)),
        ],
        compiler_params=pltpu.CompilerParams(
            collective_id=0, has_side_effects=True, vmem_limit_bytes=56 * 2**20
        ),
    )(queries, keys, values, grad_out, out_weight, doc_lengths, strata, mask_level)


def solution(mesh):
    placed = (
        P("ctx", "head"),
        P("ctx", "head"),
        P("ctx", "head"),
        P("ctx", "head"),
        P(None, "head"),
        P(),
        P(),
        P("ctx"),
    )
    return jax.shard_map(
        local,
        mesh=mesh,
        in_specs=placed,
        out_specs=(P("ctx", "head"), P("ctx", "head"), P("ctx", "head"), P("ctx", "head")),
        check_vma=False,
    )
```

time: 341 us -> 69.4 us (0.20)
  the two profiles are of different devices: /device:TPU:16 before, /device:TPU:10 now
where the time goes in v1:
time: 69.4 us; the launch traced here: 69.2 us
  Pallas kernels  62.3 us (90%)
  local copies, waits for them, and re-layouts  6.27 us (9%)
    pallas_call x1, Pallas kernels, local(): pl.pallas_call(kernel, out_shape=[jax.ShapeDtypeStruct((TOK, COLS), BF16)...  62.3 us
    unnamed x4, local copies, waits for them, and re-layouts  6.27 us

profile of v1, /device:TPU:10, one launch (start us, length us, event | category | flops | bytes accessed | tf_op | source)
XLA Modules:
  0.0 69.2 jit_solution(3553096867205140697)
XLA Ops:
  0.6 62.3 %shard_map.111 = (bf16[256,256]{1,0:T(8,128)(2,1)}, bf16[256,256]{1,0:T(8,128)(2,1)}, bf16[256,256]{1,0:T(8,128)(2,1)}, f32[128,256]{1,0:T(8,128)}) custom-call(bf16[256,256]{1,0:T(8,128)(2,1)} %q_hbm.1, bf16[256,256]{1,0:T(8,128)(2,1)} %k_hbm.1, bf16[256,256]{1,0:T(8,128)(2,1)} %v_hbm.1, bf16[256,256]{1,0:T(8,128)(2,1)} %g_hbm.1, bf16[4096,256]{1,0:T(8,128)(2,1)} %w_hbm.1, ...), custom_call_target="tpu_custom_call" | custom-call | tf_op jit(solution)/shard_map/pallas_call | solution.py:381
  62.9 1.6 %copy.16 = bf16[256,256]{1,0:T(8,128)(2,1)} copy(bf16[256,256]{1,0:T(8,128)(2,1)} %get-tuple-element.8) | data formatting | bytes 262144
  64.5 1.6 %copy.17 = bf16[256,256]{1,0:T(8,128)(2,1)} copy(bf16[256,256]{1,0:T(8,128)(2,1)} %get-tuple-element.9) | data formatting | bytes 262144
  66.1 1.6 %copy.18 = bf16[256,256]{1,0:T(8,128)(2,1)} copy(bf16[256,256]{1,0:T(8,128)(2,1)} %get-tuple-element.10) | data formatting | bytes 262144
  67.6 1.6 %copy.19 = f32[128,256]{1,0:T(8,128)} copy(f32[128,256]{1,0:T(8,128)} %get-tuple-element.11) | data formatting | bytes 262144

commit v2 on v1

v2 whole, which is shorter than its diff:
```python
import jax
import jax.numpy as jnp
from jax import lax
from jax.experimental import pallas as pl
from jax.experimental.pallas import tpu as pltpu
from jax.sharding import PartitionSpec as P

HD = 128
STRATA = 8
MESH = pl.DeviceIdType.MESH
NZ, NX, NY = 8, 4, 8
TOK = 256
COLS = 256
HALO = 16
EXT = TOK + HALO
KEYS = 640
NEG = -1e30
DEST = 4096 // (NZ * NX)
ROWS_Z = 64
ROWS_X = DEST - ROWS_Z

NT = (((1,), (1,)), ((), ()))
TN = (((0,), (0,)), ((), ()))
F32 = jnp.float32
BF16 = jnp.bfloat16


def dot(a, b, dims=(((1,), (0,)), ((), ()))):
    return lax.dot_general(a, b, dims, preferred_element_type=F32)


def kernel(
    q_hbm, k_hbm, v_hbm, g_hbm, w_hbm, len_hbm, strata_hbm, level_hbm,
    dq_out, dk_out, dv_out, dw_out,
    len_ref, strata_ref, level_ref,
    q_all, k_all, v_all, g_all, w_all, dacc, do_all, p_all, o_all, s_all,
    dq_all, dkv_own, o_ret, ret1, ret1_in, ret2, ret2_in, part, part_in,
    parts, zs, zr, xs0, xr0, xs1, xr1, z_out, z_in, x_out, x_in, total,
    local_sem, ag_send, ag_recv, sib_send, sib_recv, kv_send, kv_recv,
    ret_send, ret_recv, z_send, z_recv, x_send, x_recv, far_send, far_recv,
):
    c = lax.axis_index("ctx")
    h = lax.axis_index("head")
    z, x, y, core = c // NX, c % NX, h // 2, h % 2
    side = c % 2
    sign = 2 * side - 1
    edge = pl.multiple_of(side * (TOK - HALO), HALO)

    def at_ctx(index):
        return {"ctx": (index + NZ * NX) % (NZ * NX), "head": h}

    def at_zx(zz, xx):
        return {"ctx": (zz + NZ) % NZ * NX + (xx + NX) % NX, "head": h}

    def at_y(yy):
        return {"ctx": c, "head": (yy + NY) % NY * 2 + core}

    y_up, y_dn = at_y(y + 1), at_y(y - 1)
    z_up, z_dn = at_zx(z + 1, x), at_zx(z - 1, x)
    x_up, x_dn = at_zx(z, x + 1), at_zx(z, x - 1)
    sibling = {"ctx": c, "head": h + 1 - 2 * core}
    partner = at_ctx(c - sign)
    mirror = at_ctx(c + sign)
    far_to, far_from = at_ctx(c + 2 * sign), at_ctx(c - 2 * sign)

    def remote(src, dst, ssem, rsem, device):
        return pltpu.make_async_remote_copy(
            src_ref=src, dst_ref=dst, send_sem=ssem, recv_sem=rsem, device_id=device, device_id_type=MESH
        )

    barrier = pltpu.get_barrier_semaphore()
    greeted = [y_up, y_dn, sibling, partner, mirror, far_to, far_from]
    greeted += [at_zx(z, x + d) for d in range(1, NX)] + [at_zx(z + d, x) for d in range(1, NZ)]
    for device in greeted:
        pl.semaphore_signal(barrier, inc=1, device_id=device, device_id_type=MESH)

    own = [
        pltpu.make_async_copy(src, dst, local_sem.at[n])
        for n, (src, dst) in enumerate(
            [
                (len_hbm, len_ref),
                (strata_hbm, strata_ref),
                (level_hbm, level_ref),
                (g_hbm, g_all.at[0, 0]),
                (q_hbm, q_all.at[pl.ds(0, TOK)]),
                (k_hbm, k_all.at[pl.ds(0, TOK)]),
                (v_hbm, v_all.at[pl.ds(0, TOK)]),
                (w_hbm, w_all),
            ]
        )
    ]
    for copy in own:
        copy.start()

    pl.semaphore_wait(barrier, len(greeted))

    half = TOK // 2

    def ag_copy(up, s, part_index, from_own):
        rows_of = pl.ds(part_index * half, half)
        direction = 0 if up else 1
        slot_here = (NY - (s - 1)) % NY if up else s - 1
        slot_there = NY - s if up else s
        src = g_hbm.at[rows_of] if from_own else g_all.at[slot_here, 0, rows_of]
        index = direction * 8 + (s - 1) * 2 + part_index
        return remote(
            src, g_all.at[slot_there, 0, rows_of], ag_send.at[index], ag_recv.at[index], y_up if up else y_dn
        )

    def sib_copy(slot):
        return remote(
            g_all.at[slot, 0] if slot else g_hbm, g_all.at[slot, 1], sib_send.at[slot], sib_recv.at[slot], sibling
        )

    ag = {}
    sib = {}
    for part_index in range(2):
        for up in (True, False):
            ag[up, 1, part_index] = ag_copy(up, 1, part_index, True)
            ag[up, 1, part_index].start()
    kv = [
        remote(k_hbm, k_all.at[pl.ds(TOK, TOK)], kv_send.at[0], kv_recv.at[0], partner),
        remote(v_hbm, v_all.at[pl.ds(TOK, TOK)], kv_send.at[1], kv_recv.at[1], partner),
    ]
    rim = pl.ds(edge, HALO)
    for n, (src, dst, device) in enumerate(
        [
            (k_hbm, k_all.at[pl.ds(2 * TOK, HALO)], mirror),
            (v_hbm, v_all.at[pl.ds(2 * TOK, HALO)], mirror),
            (q_hbm, q_all.at[pl.ds(TOK, HALO)], mirror),
            (k_hbm, k_all.at[pl.ds(2 * TOK + HALO, HALO)], far_to),
            (v_hbm, v_all.at[pl.ds(2 * TOK + HALO, HALO)], far_to),
        ]
    ):
        kv.append(remote(src.at[rim], dst, kv_send.at[2 + n], kv_recv.at[2 + n], device))
    for copy in kv[2:] + kv[:2]:
        copy.start()
    def pass_on(slot):
        sib[slot] = sib_copy(slot)
        sib[slot].start()

    pass_on(0)

    for copy in own:
        copy.wait()

    doc = c // 2
    position = c * TOK + lax.broadcasted_iota(jnp.int32, (1, TOK), 1)
    stratum = jnp.zeros((1, TOK), jnp.int32)
    begin = jnp.int32(0)
    doc_begin = jnp.int32(0)
    doc_end = jnp.int32(0)
    for n in range(16):
        finish = begin + len_ref[n]
        within = (position >= begin) & (position < finish)
        stratum = jnp.where(within, strata_ref[n], stratum)
        doc_begin = jnp.where(doc == n, begin, doc_begin)
        doc_end = jnp.where(doc == n, finish, doc_end)
        begin = finish
    level = level_ref[...].reshape(1, TOK)
    weight_row = jnp.where(level < stratum + 1, STRATA / (stratum + 1).astype(F32), 0.0)
    weight = jnp.transpose(jnp.broadcast_to(weight_row, (HD, TOK)))

    other = 1 - side

    def place(index, own_first, halo_first):
        return jnp.where(index < TOK, own_first + index, halo_first + index - TOK)

    own_first = c * TOK
    own_halo = own_first - HALO + (TOK + HALO) * side
    partner_first = (c - sign) * TOK
    partner_halo = partner_first - HALO + (TOK + HALO) * other
    rows = place(lax.broadcasted_iota(jnp.int32, (EXT, 1), 0), own_first, own_halo)
    row_in = ((rows >= doc_begin) & (rows < doc_end)).astype(F32)
    lane = lax.broadcasted_iota(jnp.int32, (1, KEYS), 1)
    keys_at = jnp.where(
        lane < TOK,
        own_first + lane,
        jnp.where(
            lane < 2 * TOK,
            partner_first + lane - TOK,
            jnp.where(lane < 2 * TOK + HALO, own_halo + lane - 2 * TOK, partner_halo + lane - 2 * TOK - HALO),
        ),
    )
    key_in = (keys_at >= doc_begin) & (keys_at < doc_end) & (lane < 2 * TOK + 2 * HALO)
    bias = jnp.where(key_in, 0.0, NEG)
    pad = KEYS - 2 * TOK - 2 * HALO
    k_all[pl.ds(KEYS - pad, pad), :] = jnp.zeros((pad, COLS), BF16)
    v_all[pl.ds(KEYS - pad, pad), :] = jnp.zeros((pad, COLS), BF16)

    def ag_step(s):
        for part_index in range(2):
            for up in (True, False):
                ag[up, s, part_index].wait_recv()
                if s + 1 < NY // 2 or part_index == (0 if up else 1):
                    ag[up, s + 1, part_index] = ag_copy(up, s + 1, part_index, False)
                    ag[up, s + 1, part_index].start()
        pass_on(NY - s)
        pass_on(s)

    ag_step(1)
    ag_step(2)

    scale = HD**-0.5
    for copy in kv:
        copy.wait_recv()

    def forward(n, first, count):
        rows_of, cols = pl.ds(first, count), pl.ds(n * HD, HD)
        scores = dot(q_all[rows_of, cols], k_all[:, cols], NT) * scale + bias
        top = jnp.max(scores, axis=1, keepdims=True)
        terms = jnp.exp(scores - top)
        attention = terms * (row_in[first : first + count] / jnp.sum(terms, axis=1, keepdims=True))
        p_all[n, rows_of, :] = attention
        o_all[rows_of, cols] = dot(attention.astype(BF16), v_all[:, cols])

    forward(0, TOK, HALO)
    forward(1, TOK, HALO)
    back = remote(o_all.at[pl.ds(TOK, HALO)], o_ret, ret_send.at[0], ret_recv.at[0], mirror)
    back.start()
    forward(0, 0, TOK)
    forward(1, 0, TOK)

    ag_step(3)

    back.wait_recv()
    s_all[...] = o_all[pl.ds(0, TOK), :]
    s_all[rim, :] += o_ret[...]
    for n in range(2):
        cols = pl.ds(n * HD, HD)
        s_all[:, cols] = s_all[:, cols] * weight
    scaled = s_all[...].astype(BF16)

    spots = [(x + 2) % NX, (x + 1) % NX, (x + NX - 1) % NX, x]

    def make_part(d):
        if d:
            sib[d].wait_recv()
        for r in range(2):
            first = (y + d) % NY * (2 * COLS) + (core + r) % 2 * COLS
            parts[pl.ds(pl.multiple_of(first, COLS), COLS), :] = dot(g_all[d, r], scaled, TN)

    def part_z(e, q):
        first = (z + e) % NZ * (NX * DEST) + spots[q] * DEST
        return parts[pl.ds(pl.multiple_of(first, DEST), ROWS_Z), :]

    def part_x(d, q):
        first = (y + d) % NY * (NX * DEST) + spots[q] * DEST + ROWS_Z
        return parts[pl.ds(pl.multiple_of(first, 16), ROWS_X), :]

    zc = {}

    def z_send_slot(up, t, q):
        e = 4 - t if up else (4 + t) % NZ
        value = part_z(e, q)
        d = 0 if up else 1
        if (up, t - 1, q) in zc:
            zc[up, t - 1, q].wait_recv()
            value = value + zr[d, t - 1, q].astype(F32)
        zs[d, t, q] = value.astype(BF16)
        index = d * 16 + t * 4 + q
        zc[up, t, q] = remote(
            zs.at[d, t, q], zr.at[d, t, q], z_send.at[index], z_recv.at[index], z_up if up else z_dn
        )
        zc[up, t, q].start()

    def z_first(t):
        for q in range(2):
            z_send_slot(True, t, q)
            z_send_slot(False, t, q + 2)

    def z_second(t):
        for q in range(2):
            z_send_slot(True, t, q + 2)
            z_send_slot(False, t, q)

    xc = {}
    pairs = ((0, 1), (7, 2), (6, 3), (5, 4))

    def x_start(u):
        for n, up in enumerate((True, False)):
            xs0[u, n] = part_x(pairs[u][n], 0).astype(BF16)
            index = u * 2 + n
            xc[up, 0, u] = remote(
                xs0.at[u, n], xr0.at[u, n], x_send.at[index], x_recv.at[index], x_up if up else x_dn
            )
            xc[up, 0, u].start()

    def x_next(u):
        for n, up in enumerate((True, False)):
            for m in range(2):
                value = part_x(pairs[u][m], 1 if up else 2)
                if m == n:
                    xc[up, 0, u].wait_recv()
                    value = value + xr0[u, n].astype(F32)
                xs1[u, n, m] = value.astype(BF16)
            index = 8 + u * 2 + n
            xc[up, 1, u] = remote(
                xs1.at[u, n], xr1.at[u, n], x_send.at[index], x_recv.at[index], x_up if up else x_dn
            )
            xc[up, 1, u].start()

    straight = []

    def to_z(d):
        e = (y + d - z + NZ) % NZ
        return e, remote(z_out.at[d], z_in.at[e], far_send.at[d], far_recv.at[e], at_zx(y + d, x))

    def to_z_in(e):
        return remote(z_out.at[0], z_in.at[e], far_send.at[0], far_recv.at[e], at_zx(z + e, x))

    def x_total(u):
        for up in (True, False):
            xc[up, 1, u].wait_recv()
        for m, d in enumerate(pairs[u]):
            value = part_x(d, 3) + xr1[u, 0, m].astype(F32) + xr1[u, 1, m].astype(F32)
            z_out[d] = value.astype(BF16)
            e, copy = to_z(d)

            @pl.when(e != 0)
            def _():
                copy.start()

            @pl.when(e == 0)
            def _():
                total[pl.ds(ROWS_Z, ROWS_X), :] = value

    sib[0].wait_recv()
    for d in (0, 1, 7, 2):
        make_part(d)
    x_start(0)
    x_start(1)
    for d in (6, 3):
        make_part(d)
    x_start(2)
    last = NY // 2
    for up in (True, False):
        ag[up, last, 0 if up else 1].wait_recv()
    pass_on(last)
    x_next(0)
    x_next(1)
    make_part(5)
    make_part(4)
    z_first(0)
    x_start(3)
    z_second(1)

    dacc[...] = jnp.zeros((TOK, COLS), F32)
    for slot in range(NY):
        for r in range(2):
            index = (y + slot) % NY * 2 + (core + r) % 2
            first = pl.multiple_of(index * COLS, COLS)
            dacc[...] += dot(g_all[slot, r], w_all[pl.ds(first, COLS), :])
    for n in range(2):
        cols = pl.ds(n * HD, HD)
        do_all[pl.ds(0, TOK), cols] = (dacc[:, cols] * weight).astype(BF16)
    halo_grad = remote(
        do_all.at[rim], do_all.at[pl.ds(TOK, HALO)], ret_send.at[1], ret_recv.at[1], mirror
    )
    halo_grad.start()

    z_first(1)
    x_next(2)
    z_second(2)
    x_next(3)

    halo_grad.wait_recv()

    def backward(n):
        cols = pl.ds(n * HD, HD)
        attention = p_all[n]
        grads = do_all[:, cols]
        correction = jnp.sum(grads.astype(F32) * o_all[:, cols], axis=1, keepdims=True)
        dots = dot(grads, v_all[:, cols], NT)
        score_grad = (attention * (dots - correction) * scale).astype(BF16)
        dq_all[:, cols] = dot(score_grad, k_all[:, cols])
        for which, value in enumerate(
            (dot(score_grad, q_all[:, cols], TN), dot(attention.astype(BF16), grads, TN))
        ):
            dkv_own[which, :, cols] = value[:TOK]
            part[which, :, cols] = value[TOK : 2 * TOK].astype(BF16)
            ret1[1 + which, :, cols] = value[2 * TOK : 2 * TOK + HALO]
            ret2[which, :, cols] = value[2 * TOK + HALO : 2 * TOK + 2 * HALO]

    x_total(0)
    x_total(1)
    backward(0)
    z_first(2)
    backward(1)
    ret1[0] = dq_all[pl.ds(TOK, HALO), :]
    returns = [
        remote(part, part_in, ret_send.at[2], ret_recv.at[2], partner),
        remote(ret1, ret1_in, ret_send.at[3], ret_recv.at[3], mirror),
        remote(ret2, ret2_in, ret_send.at[4], ret_recv.at[4], far_from),
    ]
    for copy in returns:
        copy.start()

    z_second(3)
    x_total(2)
    x_total(3)
    z_first(3)

    def z_total(q):
        for up in (True, False):
            zc[up, 3, q].wait_recv()
        return part_z(0, q) + zr[0, 3, q].astype(F32) + zr[1, 3, q].astype(F32)

    for copy in returns:
        copy.wait_recv()
    dq_all[rim, :] += ret1_in[0]
    dq_out[...] = dq_all[pl.ds(0, TOK), :].astype(BF16)
    for which, out in enumerate((dk_out, dv_out)):
        dkv_own[which, rim, :] += ret1_in[1 + which] + ret2_in[which]
        out[...] = (dkv_own[which] + part_in[which].astype(F32)).astype(BF16)

    for q, d in ((0, 2), (1, 1), (2, NX - 1)):
        x_out[q] = z_total(q).astype(BF16)
        copy = remote(x_out.at[q], x_in.at[q], far_send.at[NZ + q], far_recv.at[NZ + q], at_zx(z, x + d))
        copy.start()
        straight.append(copy)
    total[pl.ds(0, ROWS_Z), :] = z_total(3)
    for e in range(1, NZ):
        to_z_in(e).wait_recv()
    for copy in straight:
        copy.wait_recv()
    for q in range(3):
        total[pl.ds(0, ROWS_Z), :] += x_in[q].astype(F32)
    for e in range(1, NZ):
        total[pl.ds(ROWS_Z, ROWS_X), :] += z_in[e].astype(F32)
    dw_out[...] = total[...]

    for copy in list(ag.values()) + list(sib.values()) + kv + [back, halo_grad] + returns + list(zc.values()):
        copy.wait_send()
    for copy in list(xc.values()) + straight:
        copy.wait_send()
    for d in range(NZ):
        e, copy = to_z(d)

        @pl.when(e != 0)
        def _(copy=copy):
            copy.wait_send()


def tail(*refs):
    count = len(refs) // 2
    sems = refs[-1]
    copies = [pltpu.make_async_copy(refs[n], refs[count + n], sems.at[n]) for n in range(count)]
    for copy in copies:
        copy.start()
    for copy in copies:
        copy.wait()


def local(queries, keys, values, grad_out, out_weight, doc_lengths, strata, mask_level):
    hbm = pl.BlockSpec(memory_space=pl.ANY)
    vmem = pl.BlockSpec(memory_space=pltpu.VMEM)
    dma = pltpu.SemaphoreType.DMA
    V = pltpu.VMEM
    outs = pl.pallas_call(
        kernel,
        out_shape=[
            V((TOK, COLS), BF16),
            V((TOK, COLS), BF16),
            V((TOK, COLS), BF16),
            V((DEST, COLS), F32),
        ],
        in_specs=[hbm] * 8,
        out_specs=[vmem] * 4,
        scratch_shapes=[
            pltpu.SMEM((16,), jnp.int32),
            pltpu.SMEM((16,), jnp.int32),
            V((TOK,), jnp.int32),
            V((EXT, COLS), BF16),
            V((KEYS, COLS), BF16),
            V((KEYS, COLS), BF16),
            V((NY, 2, TOK, COLS), BF16),
            V((4096, COLS), BF16),
            V((TOK, COLS), F32),
            V((EXT, COLS), BF16),
            V((2, EXT, KEYS), F32),
            V((EXT, COLS), F32),
            V((TOK, COLS), F32),
            V((EXT, COLS), F32),
            V((2, TOK, COLS), F32),
            V((HALO, COLS), F32),
            V((3, HALO, COLS), F32),
            V((3, HALO, COLS), F32),
            V((2, HALO, COLS), F32),
            V((2, HALO, COLS), F32),
            V((2, TOK, COLS), BF16),
            V((2, TOK, COLS), BF16),
            V((NZ * NX * DEST, COLS), F32),
            V((2, 4, 4, ROWS_Z, COLS), BF16),
            V((2, 4, 4, ROWS_Z, COLS), BF16),
            V((4, 2, ROWS_X, COLS), BF16),
            V((4, 2, ROWS_X, COLS), BF16),
            V((4, 2, 2, ROWS_X, COLS), BF16),
            V((4, 2, 2, ROWS_X, COLS), BF16),
            V((NZ, ROWS_X, COLS), BF16),
            V((NZ, ROWS_X, COLS), BF16),
            V((3, ROWS_Z, COLS), BF16),
            V((3, ROWS_Z, COLS), BF16),
            V((DEST, COLS), F32),
            dma((8,)),
            dma((16,)),
            dma((16,)),
            dma((8,)),
            dma((8,)),
            dma((7,)),
            dma((7,)),
            dma((5,)),
            dma((5,)),
            dma((32,)),
            dma((32,)),
            dma((16,)),
            dma((16,)),
            dma((NZ + 3,)),
            dma((NZ + 3,)),
        ],
        compiler_params=pltpu.CompilerParams(
            collective_id=0, has_side_effects=True, vmem_limit_bytes=60 * 2**20
        ),
    )(queries, keys, values, grad_out, out_weight, doc_lengths, strata, mask_level)
    return pl.pallas_call(
        tail,
        out_shape=[jax.ShapeDtypeStruct(a.shape, a.dtype) for a in outs],
        in_specs=[vmem] * 4,
        out_specs=[hbm] * 4,
        scratch_shapes=[dma((4,))],
        compiler_params=pltpu.CompilerParams(vmem_limit_bytes=8 * 2**20),
    )(*outs)


def solution(mesh):
    placed = (
        P("ctx", "head"),
        P("ctx", "head"),
        P("ctx", "head"),
        P("ctx", "head"),
        P(None, "head"),
        P(),
        P(),
        P("ctx"),
    )
    return jax.shard_map(
        local,
        mesh=mesh,
        in_specs=placed,
        out_specs=(P("ctx", "head"), P("ctx", "head"), P("ctx", "head"), P("ctx", "head")),
        check_vma=False,
    )
```

time: 69.4 us -> 59.2 us (0.85)
  the two profiles are of different devices: /device:TPU:10 before, /device:TPU:1 now
where the time goes in v2:
time: 59.2 us; the launch traced here: 59.1 us
  Pallas kernels  58.5 us (99%)
  between operations  0.64 us (1%)
    pallas_call x1, Pallas kernels, local(): pl.pallas_call(kernel, out_shape=[V((TOK, COLS), BF16), V((TOK, COLS), BF...  57.6 us

profile of v2, /device:TPU:1, one launch (start us, length us, event | category | flops | bytes accessed | tf_op | source)
XLA Modules:
  0.0 59.1 jit_solution(6443524120380728788)
XLA Ops:
  0.6 57.6 %shard_map.111 = (bf16[256,256]{1,0:T(8,128)(2,1)S(1)}, bf16[256,256]{1,0:T(8,128)(2,1)S(1)}, bf16[256,256]{1,0:T(8,128)(2,1)S(1)}, f32[128,256]{1,0:T(8,128)S(1)}) custom-call(bf16[256,256]{1,0:T(8,128)(2,1)} %q_hbm.1, bf16[256,256]{1,0:T(8,128)(2,1)} %k_hbm.1, bf16[256,256]{1,0:T(8,128)(2,1)} %v_hbm.1, bf16[256,256]{1,0:T(8,128)(2,1)} %g_hbm.1, ...), custom_call_target="tpu_custom_call" | custom-call | tf_op jit(solution)/shard_map/pallas_call | solution.py:460
  58.3 0.8 %shard_map.112 = (bf16[256,256]{1,0:T(8,128)(2,1)}, bf16[256,256]{1,0:T(8,128)(2,1)}, bf16[256,256]{1,0:T(8,128)(2,1)}, f32[128,256]{1,0:T(8,128)}) custom-call(bf16[256,256]{1,0:T(8,128)(2,1)S(1)} %get-tuple-element.8.refs_0_, bf16[256,256]{1,0:T(8,128)(2,1)S(1)} %get-tuple-element.9.refs_1_, bf16[256,256]{1,0:T(8,128)(2,1)S(1)} %get-tuple-element.10.refs_2_, ...), custom_call_target="tpu_custom_call" | custom-call | tf_op jit(solution)/shard_map/pallas_call | solution.py:525

commit v3 on v2

--- a/solution.py
+++ b/solution.py
@@ -35,7 +35,7 @@
     len_ref, strata_ref, level_ref,
     q_all, k_all, v_all, g_all, w_all, dacc, do_all, p_all, o_all, s_all,
     dq_all, dkv_own, o_ret, ret1, ret1_in, ret2, ret2_in, part, part_in,
-    parts, zs, zr, xs0, xr0, xs1, xr1, z_out, z_in, x_out, x_in, total,
+    parts, zs, zr, xs0, xr0, xs1, xr1, totals, z_sum, z_out, z_in, x_out, x_in, total,
     local_sem, ag_send, ag_recv, sib_send, sib_recv, kv_send, kv_recv,
     ret_send, ret_recv, z_send, z_recv, x_send, x_recv, far_send, far_recv,
 ):
@@ -52,10 +52,9 @@
     def at_zx(zz, xx):
         return {"ctx": (zz + NZ) % NZ * NX + (xx + NX) % NX, "head": h}
 
-    def at_y(yy):
-        return {"ctx": c, "head": (yy + NY) % NY * 2 + core}
-
-    y_up, y_dn = at_y(y + 1), at_y(y - 1)
+    def at_y(yy, k):
+        return {"ctx": c, "head": (yy + NY) % NY * 2 + k}
+
     z_up, z_dn = at_zx(z + 1, x), at_zx(z - 1, x)
     x_up, x_dn = at_zx(z, x + 1), at_zx(z, x - 1)
     sibling = {"ctx": c, "head": h + 1 - 2 * core}
@@ -69,7 +68,7 @@
         )
 
     barrier = pltpu.get_barrier_semaphore()
-    greeted = [y_up, y_dn, sibling, partner, mirror, far_to, far_from]
+    greeted = [at_y(y + d, k) for d in (1, -1) for k in range(2)] + [sibling, partner, mirror, far_to, far_from]
     greeted += [at_zx(z, x + d) for d in range(1, NX)] + [at_zx(z + d, x) for d in range(1, NZ)]
     for device in greeted:
         pl.semaphore_signal(barrier, inc=1, device_id=device, device_id_type=MESH)
@@ -81,7 +80,7 @@
                 (len_hbm, len_ref),
                 (strata_hbm, strata_ref),
                 (level_hbm, level_ref),
-                (g_hbm, g_all.at[0, 0]),
+                (g_hbm, g_all.at[0, core]),
                 (q_hbm, q_all.at[pl.ds(0, TOK)]),
                 (k_hbm, k_all.at[pl.ds(0, TOK)]),
                 (v_hbm, v_all.at[pl.ds(0, TOK)]),
@@ -94,30 +93,45 @@
 
     pl.semaphore_wait(barrier, len(greeted))
 
-    half = TOK // 2
-
-    def ag_copy(up, s, part_index, from_own):
-        rows_of = pl.ds(part_index * half, half)
-        direction = 0 if up else 1
-        slot_here = (NY - (s - 1)) % NY if up else s - 1
-        slot_there = NY - s if up else s
-        src = g_hbm.at[rows_of] if from_own else g_all.at[slot_here, 0, rows_of]
-        index = direction * 8 + (s - 1) * 2 + part_index
+    chunk = TOK // 4
+
+    def chunk_at(p, k):
+        return pl.ds(pl.multiple_of((p + 2 * k) % 4 * chunk, chunk), chunk)
+
+    ag = []
+
+    def ag_first(p, up):
+        rows_of = chunk_at(p, 0 if up else 1)
+        copy = remote(
+            g_hbm.at[rows_of], g_all.at[NY - 1 if up else 1, core, rows_of],
+            ag_send.at[p if up else 4 + p], ag_recv.at[core * 4 + p],
+            at_y(y + 1, 0) if up else at_y(y - 1, 1),
+        )
+        copy.start()
+        ag.append(copy)
+
+    onward = at_y(y + 1 - 2 * core, core)
+
+    def slot_at(s):
+        return (NY + (2 * core - 1) * s) % NY
+
+    def ag_copy(s, k, p):
+        rows_of = chunk_at(p, core)
+        index = 8 * s + 4 * k + p
         return remote(
-            src, g_all.at[slot_there, 0, rows_of], ag_send.at[index], ag_recv.at[index], y_up if up else y_dn
+            g_all.at[slot_at(s), k, rows_of], g_all.at[slot_at(s + 1), k, rows_of],
+            ag_send.at[index], ag_recv.at[index], onward,
         )
 
-    def sib_copy(slot):
-        return remote(
-            g_all.at[slot, 0] if slot else g_hbm, g_all.at[slot, 1], sib_send.at[slot], sib_recv.at[slot], sibling
-        )
-
-    ag = {}
-    sib = {}
-    for part_index in range(2):
+    def ag_arrival(s, k, p):
+        rows_of = chunk_at(p, core)
+        index = 8 * (s - 1) + 4 * k + p
+        here = g_all.at[slot_at(s), k, rows_of]
+        remote(here, here, ag_send.at[index], ag_recv.at[index], onward).wait_recv()
+
+    for p in range(4):
         for up in (True, False):
-            ag[up, 1, part_index] = ag_copy(up, 1, part_index, True)
-            ag[up, 1, part_index].start()
+            ag_first(p, up)
     kv = [
         remote(k_hbm, k_all.at[pl.ds(TOK, TOK)], kv_send.at[0], kv_recv.at[0], partner),
         remote(v_hbm, v_all.at[pl.ds(TOK, TOK)], kv_send.at[1], kv_recv.at[1], partner),
@@ -135,9 +149,27 @@
         kv.append(remote(src.at[rim], dst, kv_send.at[2 + n], kv_recv.at[2 + n], device))
     for copy in kv[2:] + kv[:2]:
         copy.start()
-    def pass_on(slot):
-        sib[slot] = sib_copy(slot)
-        sib[slot].start()
+    sib = []
+
+    def pass_on(s):
+        if s == 0:
+            src, dst = g_hbm, g_all.at[0, core]
+        elif s < NY // 2:
+            src = dst = g_all.at[slot_at(s)]
+        else:
+            src = dst = g_all.at[s, :, pl.ds(pl.multiple_of(core * (TOK // 2), TOK // 2), TOK // 2)]
+        copy = remote(src, dst, sib_send.at[s], sib_recv.at[s], sibling)
+        copy.start()
+        sib.append(copy)
+
+    def from_sibling(s):
+        if s == 0:
+            here = g_all.at[0, 1 - core]
+        elif s < NY // 2:
+            here = g_all.at[slot_at(-s)]
+        else:
+            here = g_all.at[s, :, pl.ds(pl.multiple_of((1 - core) * (TOK // 2), TOK // 2), TOK // 2)]
+        remote(here, here, sib_send.at[s], sib_recv.at[s], sibling).wait_recv()
 
     pass_on(0)
 
@@ -189,13 +221,13 @@
     v_all[pl.ds(KEYS - pad, pad), :] = jnp.zeros((pad, COLS), BF16)
 
     def ag_step(s):
-        for part_index in range(2):
-            for up in (True, False):
-                ag[up, s, part_index].wait_recv()
-                if s + 1 < NY // 2 or part_index == (0 if up else 1):
-                    ag[up, s + 1, part_index] = ag_copy(up, s + 1, part_index, False)
-                    ag[up, s + 1, part_index].start()
-        pass_on(NY - s)
+        for p in range(4 if s < NY // 2 else 2):
+            for k in range(2):
+                ag_arrival(s, k, p)
+                if s < NY // 2 and (s + 1 < NY // 2 or p < 2):
+                    copy = ag_copy(s, k, p)
+                    copy.start()
+                    ag.append(copy)
         pass_on(s)
 
     ag_step(1)
@@ -234,10 +266,8 @@
     spots = [(x + 2) % NX, (x + 1) % NX, (x + NX - 1) % NX, x]
 
     def make_part(d):
-        if d:
-            sib[d].wait_recv()
         for r in range(2):
-            first = (y + d) % NY * (2 * COLS) + (core + r) % 2 * COLS
+            first = (y + d) % NY * (2 * COLS) + r * COLS
             parts[pl.ds(pl.multiple_of(first, COLS), COLS), :] = dot(g_all[d, r], scaled, TN)
 
     def part_z(e, q):
@@ -250,29 +280,31 @@
 
     zc = {}
 
-    def z_send_slot(up, t, q):
+    def z_send_group(up, t, late):
         e = 4 - t if up else (4 + t) % NZ
-        value = part_z(e, q)
-        d = 0 if up else 1
-        if (up, t - 1, q) in zc:
-            zc[up, t - 1, q].wait_recv()
-            value = value + zr[d, t - 1, q].astype(F32)
-        zs[d, t, q] = value.astype(BF16)
-        index = d * 16 + t * 4 + q
-        zc[up, t, q] = remote(
-            zs.at[d, t, q], zr.at[d, t, q], z_send.at[index], z_recv.at[index], z_up if up else z_dn
+        d, group = 0 if up else 1, 0 if up != late else 1
+        came = zc.get((up, t - 1, late))
+        if came is not None:
+            came.wait_recv()
+        for n in range(2):
+            value = part_z(e, group * 2 + n)
+            if came is not None:
+                value = value + zr[d, t - 1, group, n].astype(F32)
+            zs[d, t, group, n] = value.astype(BF16)
+        index = d * 8 + t * 2 + group
+        copy = remote(
+            zs.at[d, t, group], zr.at[d, t, group], z_send.at[index], z_recv.at[index], z_up if up else z_dn
         )
-        zc[up, t, q].start()
+        copy.start()
+        zc[up, t, late] = copy
 
     def z_first(t):
-        for q in range(2):
-            z_send_slot(True, t, q)
-            z_send_slot(False, t, q + 2)
+        z_send_group(True, t, False)
+        z_send_group(False, t, False)
 
     def z_second(t):
-        for q in range(2):
-            z_send_slot(True, t, q + 2)
-            z_send_slot(False, t, q)
+        z_send_group(True, t, True)
+        z_send_group(False, t, True)
 
     xc = {}
     pairs = ((0, 1), (7, 2), (6, 3), (5, 4))
@@ -300,57 +332,65 @@
             )
             xc[up, 1, u].start()
 
-    straight = []
-
-    def to_z(d):
-        e = (y + d - z + NZ) % NZ
-        return e, remote(z_out.at[d], z_in.at[e], far_send.at[d], far_recv.at[e], at_zx(y + d, x))
-
-    def to_z_in(e):
-        return remote(z_out.at[0], z_in.at[e], far_send.at[0], far_recv.at[e], at_zx(z + e, x))
-
     def x_total(u):
         for up in (True, False):
             xc[up, 1, u].wait_recv()
         for m, d in enumerate(pairs[u]):
-            value = part_x(d, 3) + xr1[u, 0, m].astype(F32) + xr1[u, 1, m].astype(F32)
-            z_out[d] = value.astype(BF16)
-            e, copy = to_z(d)
-
-            @pl.when(e != 0)
-            def _():
-                copy.start()
-
-            @pl.when(e == 0)
-            def _():
-                total[pl.ds(ROWS_Z, ROWS_X), :] = value
-
-    sib[0].wait_recv()
+            totals[(y + d) % NY] = part_x(d, 3) + xr1[u, 0, m].astype(F32) + xr1[u, 1, m].astype(F32)
+
+    straight = []
+
+    def over_z(n, e, first, count, hop, *more):
+        value = totals[(z + e) % NZ, first : first + count]
+        for slot in more:
+            straight[slot].wait_recv()
+            if slot < 2:
+                here = slice(0, ROWS_X // 2) if slot == 0 else slice(ROWS_X // 2, ROWS_X)
+                z_sum[...] = value
+                z_sum[here] += z_in[slot, : ROWS_X // 2].astype(F32)
+                value = z_sum[...]
+            else:
+                value = value + z_in[slot].astype(F32)
+        z_out[n, :count] = value.astype(BF16)
+        here = pl.ds(0, count)
+        copy = remote(
+            z_out.at[n, here], z_in.at[n, here], far_send.at[n], far_recv.at[n], at_zx(z + hop, x)
+        )
+        copy.start()
+        straight.append(copy)
+
+    for s in range(3):
+        from_sibling(s)
     for d in (0, 1, 7, 2):
         make_part(d)
     x_start(0)
     x_start(1)
+    ag_step(NY // 2)
+    from_sibling(3)
     for d in (6, 3):
         make_part(d)
     x_start(2)
-    last = NY // 2
-    for up in (True, False):
-        ag[up, last, 0 if up else 1].wait_recv()
-    pass_on(last)
-    x_next(0)
-    x_next(1)
     make_part(5)
+
+    def grad_block(slot):
+        value = None
+        for r in range(2):
+            first = (y + slot) % NY * (2 * COLS) + r * COLS
+            term = dot(g_all[slot, r], w_all[pl.ds(pl.multiple_of(first, COLS), COLS), :])
+            value = term if value is None else value + term
+        return value
+
+    dacc[...] = grad_block(0)
+    for slot in (1, 7, 2, 6, 3, 5):
+        dacc[...] += grad_block(slot)
+
+    from_sibling(NY // 2)
     make_part(4)
     z_first(0)
     x_start(3)
     z_second(1)
 
-    dacc[...] = jnp.zeros((TOK, COLS), F32)
-    for slot in range(NY):
-        for r in range(2):
-            index = (y + slot) % NY * 2 + (core + r) % 2
-            first = pl.multiple_of(index * COLS, COLS)
-            dacc[...] += dot(g_all[slot, r], w_all[pl.ds(first, COLS), :])
+    dacc[...] += grad_block(4)
     for n in range(2):
         cols = pl.ds(n * HD, HD)
         do_all[pl.ds(0, TOK), cols] = (dacc[:, cols] * weight).astype(BF16)
@@ -359,6 +399,8 @@
     )
     halo_grad.start()
 
+    x_next(0)
+    x_next(1)
     z_first(1)
     x_next(2)
     z_second(2)
@@ -382,8 +424,6 @@
             ret1[1 + which, :, cols] = value[2 * TOK : 2 * TOK + HALO]
             ret2[which, :, cols] = value[2 * TOK + HALO : 2 * TOK + 2 * HALO]
 
-    x_total(0)
-    x_total(1)
     backward(0)
     z_first(2)
     backward(1)
@@ -397,14 +437,37 @@
         copy.start()
 
     z_second(3)
-    x_total(2)
-    x_total(3)
+    for u in range(4):
+        x_total(u)
+    mid = ROWS_X // 2
+    over_z(0, 4, 0, mid, 2)
+    over_z(1, 4, mid, mid, -2)
+    over_z(2, 3, 0, ROWS_X, 1)
+    over_z(3, 5, 0, ROWS_X, -1)
+    over_z(4, 1, 0, ROWS_X, 1)
+    over_z(5, 7, 0, ROWS_X, -1)
     z_first(3)
+    over_z(6, 2, 0, ROWS_X, 2, 0, 2)
+    over_z(7, 6, 0, ROWS_X, -2, 1, 3)
+    total[pl.ds(ROWS_Z, ROWS_X), :] = totals[z]
 
     def z_total(q):
-        for up in (True, False):
-            zc[up, 3, q].wait_recv()
-        return part_z(0, q) + zr[0, 3, q].astype(F32) + zr[1, 3, q].astype(F32)
+        value = part_z(0, q)
+        for d, up in ((0, True), (1, False)):
+            late = (q >= 2) == up
+            if (d, q // 2) not in arrived:
+                zc[up, 3, late].wait_recv()
+                arrived.add((d, q // 2))
+            value = value + zr[d, 3, q // 2, q % 2].astype(F32)
+        return value
+
+    arrived = set()
+    for q, d in ((0, 2), (1, 1), (2, NX - 1)):
+        x_out[q] = z_total(q).astype(BF16)
+        copy = remote(x_out.at[q], x_in.at[q], far_send.at[NZ + q], far_recv.at[NZ + q], at_zx(z, x + d))
+        copy.start()
+        straight.append(copy)
+    total[pl.ds(0, ROWS_Z), :] = z_total(3)
 
     for copy in returns:
         copy.wait_recv()
@@ -414,32 +477,18 @@
         dkv_own[which, rim, :] += ret1_in[1 + which] + ret2_in[which]
         out[...] = (dkv_own[which] + part_in[which].astype(F32)).astype(BF16)
 
-    for q, d in ((0, 2), (1, 1), (2, NX - 1)):
-        x_out[q] = z_total(q).astype(BF16)
-        copy = remote(x_out.at[q], x_in.at[q], far_send.at[NZ + q], far_recv.at[NZ + q], at_zx(z, x + d))
-        copy.start()
-        straight.append(copy)
-    total[pl.ds(0, ROWS_Z), :] = z_total(3)
-    for e in range(1, NZ):
-        to_z_in(e).wait_recv()
-    for copy in straight:
+    for copy in straight[4:]:
         copy.wait_recv()
+    for n in range(4, NZ):
+        total[pl.ds(ROWS_Z, ROWS_X), :] += z_in[n].astype(F32)
     for q in range(3):
         total[pl.ds(0, ROWS_Z), :] += x_in[q].astype(F32)
-    for e in range(1, NZ):
-        total[pl.ds(ROWS_Z, ROWS_X), :] += z_in[e].astype(F32)
     dw_out[...] = total[...]
 
-    for copy in list(ag.values()) + list(sib.values()) + kv + [back, halo_grad] + returns + list(zc.values()):
+    for copy in ag + sib + kv + [back, halo_grad] + returns + list(zc.values()):
         copy.wait_send()
     for copy in list(xc.values()) + straight:
         copy.wait_send()
-    for d in range(NZ):
-        e, copy = to_z(d)
-
-        @pl.when(e != 0)
-        def _(copy=copy):
-            copy.wait_send()
 
 
 def tail(*refs):
@@ -491,28 +540,30 @@
             V((2, TOK, COLS), BF16),
             V((2, TOK, COLS), BF16),
             V((NZ * NX * DEST, COLS), F32),
-            V((2, 4, 4, ROWS_Z, COLS), BF16),
-            V((2, 4, 4, ROWS_Z, COLS), BF16),
+            V((2, 4, 2, 2, ROWS_Z, COLS), BF16),
+            V((2, 4, 2, 2, ROWS_Z, COLS), BF16),
             V((4, 2, ROWS_X, COLS), BF16),
             V((4, 2, ROWS_X, COLS), BF16),
             V((4, 2, 2, ROWS_X, COLS), BF16),
             V((4, 2, 2, ROWS_X, COLS), BF16),
+            V((NZ, ROWS_X, COLS), F32),
+            V((ROWS_X, COLS), F32),
             V((NZ, ROWS_X, COLS), BF16),
             V((NZ, ROWS_X, COLS), BF16),
             V((3, ROWS_Z, COLS), BF16),
             V((3, ROWS_Z, COLS), BF16),
             V((DEST, COLS), F32),
             dma((8,)),
-            dma((16,)),
-            dma((16,)),
-            dma((8,)),
-            dma((8,)),
+            dma((32,)),
+            dma((32,)),
+            dma((5,)),
+            dma((5,)),
             dma((7,)),
             dma((7,)),
             dma((5,)),
             dma((5,)),
-            dma((32,)),
-            dma((32,)),
+            dma((16,)),
+            dma((16,)),
             dma((16,)),
             dma((16,)),
             dma((NZ + 3,)),

time: 59.2 us -> 55.6 us (0.939)
  the two profiles are of different devices: /device:TPU:1 before, /device:TPU:2 now
where the time goes in v3:
time: 55.6 us; the launch traced here: 55.5 us
  Pallas kernels  54.8 us (99%)
  between operations  0.64 us (1%)
    pallas_call x1, Pallas kernels, local(): pl.pallas_call(kernel, out_shape=[V((TOK, COLS), BF16), V((TOK, COLS), BF...  54 us

profile of v3, /device:TPU:2, one launch (start us, length us, event | category | flops | bytes accessed | tf_op | source)
XLA Modules:
  0.0 55.5 jit_solution(12915689740063586706)
XLA Ops:
  0.6 54.0 %shard_map.111 = (bf16[256,256]{1,0:T(8,128)(2,1)S(1)}, bf16[256,256]{1,0:T(8,128)(2,1)S(1)}, bf16[256,256]{1,0:T(8,128)(2,1)S(1)}, f32[128,256]{1,0:T(8,128)S(1)}) custom-call(bf16[256,256]{1,0:T(8,128)(2,1)} %q_hbm.1, bf16[256,256]{1,0:T(8,128)(2,1)} %k_hbm.1, bf16[256,256]{1,0:T(8,128)(2,1)} %v_hbm.1, bf16[256,256]{1,0:T(8,128)(2,1)} %g_hbm.1, ...), custom_call_target="tpu_custom_call" | custom-call | tf_op jit(solution)/shard_map/pallas_call | solution.py:509
  54.6 0.8 %shard_map.112 = (bf16[256,256]{1,0:T(8,128)(2,1)}, bf16[256,256]{1,0:T(8,128)(2,1)}, bf16[256,256]{1,0:T(8,128)(2,1)}, f32[128,256]{1,0:T(8,128)}) custom-call(bf16[256,256]{1,0:T(8,128)(2,1)S(1)} %get-tuple-element.8.refs_0_, bf16[256,256]{1,0:T(8,128)(2,1)S(1)} %get-tuple-element.9.refs_1_, bf16[256,256]{1,0:T(8,128)(2,1)S(1)} %get-tuple-element.10.refs_2_, ...), custom_call_target="tpu_custom_call" | custom-call | tf_op jit(solution)/shard_map/pallas_call | solution.py:576

commit v4 on v3

--- a/solution.py
+++ b/solution.py
@@ -69,7 +69,7 @@
 
     barrier = pltpu.get_barrier_semaphore()
     greeted = [at_y(y + d, k) for d in (1, -1) for k in range(2)] + [sibling, partner, mirror, far_to, far_from]
-    greeted += [at_zx(z, x + d) for d in range(1, NX)] + [at_zx(z + d, x) for d in range(1, NZ)]
+    greeted += [at_zx(z, x + d) for d in range(1, NX)] + [at_zx(z + d, x) for d in (1, 2, -2, -1)]
     for device in greeted:
         pl.semaphore_signal(barrier, inc=1, device_id=device, device_id_type=MESH)
 
@@ -220,8 +220,10 @@
     k_all[pl.ds(KEYS - pad, pad), :] = jnp.zeros((pad, COLS), BF16)
     v_all[pl.ds(KEYS - pad, pad), :] = jnp.zeros((pad, COLS), BF16)
 
-    def ag_step(s):
+    def ag_step(s, between=None):
         for p in range(4 if s < NY // 2 else 2):
+            if p == 2 and between is not None:
+                between()
             for k in range(2):
                 ag_arrival(s, k, p)
                 if s < NY // 2 and (s + 1 < NY // 2 or p < 2):
@@ -254,6 +256,7 @@
     forward(1, 0, TOK)
 
     ag_step(3)
+    ag_step(NY // 2)
 
     back.wait_recv()
     s_all[...] = o_all[pl.ds(0, TOK), :]
@@ -365,7 +368,6 @@
         make_part(d)
     x_start(0)
     x_start(1)
-    ag_step(NY // 2)
     from_sibling(3)
     for d in (6, 3):
         make_part(d)
@@ -444,9 +446,9 @@
     over_z(1, 4, mid, mid, -2)
     over_z(2, 3, 0, ROWS_X, 1)
     over_z(3, 5, 0, ROWS_X, -1)
+    z_first(3)
     over_z(4, 1, 0, ROWS_X, 1)
     over_z(5, 7, 0, ROWS_X, -1)
-    z_first(3)
     over_z(6, 2, 0, ROWS_X, 2, 0, 2)
     over_z(7, 6, 0, ROWS_X, -2, 1, 3)
     total[pl.ds(ROWS_Z, ROWS_X), :] = totals[z]

time: 55.6 us -> 54.6 us (0.982)
  Pallas kernels: 54.8 us -> 53.8 us
    pallas_call x1, Pallas kernels: 54 us -> 53 us  [local(): pl.pallas_call(kernel, out_shape=[V((TOK, COLS), BF16), V((TOK, COLS), BF...]
where the time goes in v4:
time: 54.6 us; the launch traced here: 54.5 us
  Pallas kernels  53.8 us (99%)
  between operations  0.64 us (1%)
    pallas_call x1, Pallas kernels, local(): pl.pallas_call(kernel, out_shape=[V((TOK, COLS), BF16), V((TOK, COLS), BF...  53 us

profile of v4, /device:TPU:2, one launch (start us, length us, event | category | flops | bytes accessed | tf_op | source)
XLA Modules:
  0.0 54.5 jit_solution(6696203480234522431)
XLA Ops:
  0.6 53.0 %shard_map.111 = (bf16[256,256]{1,0:T(8,128)(2,1)S(1)}, bf16[256,256]{1,0:T(8,128)(2,1)S(1)}, bf16[256,256]{1,0:T(8,128)(2,1)S(1)}, f32[128,256]{1,0:T(8,128)S(1)}) custom-call(bf16[256,256]{1,0:T(8,128)(2,1)} %q_hbm.1, bf16[256,256]{1,0:T(8,128)(2,1)} %k_hbm.1, bf16[256,256]{1,0:T(8,128)(2,1)} %v_hbm.1, bf16[256,256]{1,0:T(8,128)(2,1)} %g_hbm.1, ...), custom_call_target="tpu_custom_call" | custom-call | tf_op jit(solution)/shard_map/pallas_call | solution.py:511
  53.6 0.8 %shard_map.112 = (bf16[256,256]{1,0:T(8,128)(2,1)}, bf16[256,256]{1,0:T(8,128)(2,1)}, bf16[256,256]{1,0:T(8,128)(2,1)}, f32[128,256]{1,0:T(8,128)}) custom-call(bf16[256,256]{1,0:T(8,128)(2,1)S(1)} %get-tuple-element.8.refs_0_, bf16[256,256]{1,0:T(8,128)(2,1)S(1)} %get-tuple-element.9.refs_1_, bf16[256,256]{1,0:T(8,128)(2,1)S(1)} %get-tuple-element.10.refs_2_, ...), custom_call_target="tpu_custom_call" | custom-call | tf_op jit(solution)/shard_map/pallas_call | solution.py:578

commit v5 on v4

--- a/solution.py
+++ b/solution.py
@@ -93,10 +93,10 @@
 
     pl.semaphore_wait(barrier, len(greeted))
 
-    chunk = TOK // 4
+    chunk = TOK // 8
 
     def chunk_at(p, k):
-        return pl.ds(pl.multiple_of((p + 2 * k) % 4 * chunk, chunk), chunk)
+        return pl.ds(pl.multiple_of((p + 4 * k) % 8 * chunk, chunk), chunk)
 
     ag = []
 
@@ -104,7 +104,7 @@
         rows_of = chunk_at(p, 0 if up else 1)
         copy = remote(
             g_hbm.at[rows_of], g_all.at[NY - 1 if up else 1, core, rows_of],
-            ag_send.at[p if up else 4 + p], ag_recv.at[core * 4 + p],
+            ag_send.at[p if up else 8 + p], ag_recv.at[core * 8 + p],
             at_y(y + 1, 0) if up else at_y(y - 1, 1),
         )
         copy.start()
@@ -117,7 +117,7 @@
 
     def ag_copy(s, k, p):
         rows_of = chunk_at(p, core)
-        index = 8 * s + 4 * k + p
+        index = 16 * s + 8 * k + p
         return remote(
             g_all.at[slot_at(s), k, rows_of], g_all.at[slot_at(s + 1), k, rows_of],
             ag_send.at[index], ag_recv.at[index], onward,
@@ -125,11 +125,11 @@
 
     def ag_arrival(s, k, p):
         rows_of = chunk_at(p, core)
-        index = 8 * (s - 1) + 4 * k + p
+        index = 16 * (s - 1) + 8 * k + p
         here = g_all.at[slot_at(s), k, rows_of]
         remote(here, here, ag_send.at[index], ag_recv.at[index], onward).wait_recv()
 
-    for p in range(4):
+    for p in range(8):
         for up in (True, False):
             ag_first(p, up)
     kv = [
@@ -220,13 +220,11 @@
     k_all[pl.ds(KEYS - pad, pad), :] = jnp.zeros((pad, COLS), BF16)
     v_all[pl.ds(KEYS - pad, pad), :] = jnp.zeros((pad, COLS), BF16)
 
-    def ag_step(s, between=None):
-        for p in range(4 if s < NY // 2 else 2):
-            if p == 2 and between is not None:
-                between()
+    def ag_step(s):
+        for p in range(8 if s < NY // 2 else 4):
             for k in range(2):
                 ag_arrival(s, k, p)
-                if s < NY // 2 and (s + 1 < NY // 2 or p < 2):
+                if s < NY // 2 and (s + 1 < NY // 2 or p < 4):
                     copy = ag_copy(s, k, p)
                     copy.start()
                     ag.append(copy)
@@ -556,8 +554,8 @@
             V((3, ROWS_Z, COLS), BF16),
             V((DEST, COLS), F32),
             dma((8,)),
-            dma((32,)),
-            dma((32,)),
+            dma((64,)),
+            dma((64,)),
             dma((5,)),
             dma((5,)),
             dma((7,)),

time: 54.6 us -> 55 us (level)
  no operation moved by 1% of the time
where the time goes in v5:
time: 55 us; the launch traced here: 54.8 us
  Pallas kernels  54.2 us (99%)
  between operations  0.64 us (1%)
    pallas_call x1, Pallas kernels, local(): pl.pallas_call(kernel, out_shape=[V((TOK, COLS), BF16), V((TOK, COLS), BF...  53.4 us

profile of v5, /device:TPU:2, one launch (start us, length us, event | category | flops | bytes accessed | tf_op | source)
XLA Modules:
  0.0 54.8 jit_solution(6607898399820864045)
XLA Ops:
  0.6 53.4 %shard_map.111 = (bf16[256,256]{1,0:T(8,128)(2,1)S(1)}, bf16[256,256]{1,0:T(8,128)(2,1)S(1)}, bf16[256,256]{1,0:T(8,128)(2,1)S(1)}, f32[128,256]{1,0:T(8,128)S(1)}) custom-call(bf16[256,256]{1,0:T(8,128)(2,1)} %q_hbm.1, bf16[256,256]{1,0:T(8,128)(2,1)} %k_hbm.1, bf16[256,256]{1,0:T(8,128)(2,1)} %v_hbm.1, bf16[256,256]{1,0:T(8,128)(2,1)} %g_hbm.1, ...), custom_call_target="tpu_custom_call" | custom-call | tf_op jit(solution)/shard_map/pallas_call | solution.py:509
  54.0 0.8 %shard_map.112 = (bf16[256,256]{1,0:T(8,128)(2,1)}, bf16[256,256]{1,0:T(8,128)(2,1)}, bf16[256,256]{1,0:T(8,128)(2,1)}, f32[128,256]{1,0:T(8,128)}) custom-call(bf16[256,256]{1,0:T(8,128)(2,1)S(1)} %get-tuple-element.8.refs_0_, bf16[256,256]{1,0:T(8,128)(2,1)S(1)} %get-tuple-element.9.refs_1_, bf16[256,256]{1,0:T(8,128)(2,1)S(1)} %get-tuple-element.10.refs_2_, ...), custom_call_target="tpu_custom_call" | custom-call | tf_op jit(solution)/shard_map/pallas_call | solution.py:576
